TPU v7x, 128 devices: a whole 4x4x4 slice. The times are simulated.
128 devices in a mesh: node: 16 (over x, z), local: 8 (over y, core).
Axes of the slice: x: 4, y: 4, z: 4, core: 2. Of those that a mesh axis runs over, the one named last changes fastest.
Arguments:
- tokens: bfloat16 [16384, 2880], P(('node', 'local')), may hold values from -6 to 6
- out_grad: bfloat16 [16384, 2880], P(('node', 'local')), may hold values from -2.390625 to 2.390625
- routes: int32 [16384, 4], P(('node', 'local')), may hold values from 0 to 127, all different within a row; in each aligned block of 128 rows (0 to 127, 128 to 255, ...) at most 5 rows name the same one
- gates: float32 [16384, 4], P(('node', 'local')), may hold values from 0.1 to 1
- w_gate: bfloat16 [128, 2880, 1440], P(('node', 'local')), may hold values from -0.109375 to 0.109375
- w_up: bfloat16 [128, 2880, 1440], P(('node', 'local')), may hold values from -0.109375 to 0.109375
- w_down: bfloat16 [128, 1440, 2880], P(('node', 'local')), may hold values from -0.15625 to 0.15625
Outputs:
- input_grad: bfloat16 [16384, 2880], P(('node', 'local'))
- gate_grad: float32 [16384, 4], P(('node', 'local'))
Inputs may be any that keep to these rules, and one draw needn't show every extreme that they name: Each token names 4 different experts. Among the 128 tokens of one device (aligned blocks of rows), no expert is named by more than 5 routes, and in some such block some expert is named by exactly 5.
All inputs are finite; a program needn't handle non-finite values.
Results may differ from a plain program's by a relative error of at most 0.005.
Values may be sent and summed in bfloat16 or wider, within the bound.
No kernel may reach another device: no remote copies, remote signals or barrier semaphores. Data moves between devices by JAX's collectives and lax.ppermute only.
A program may use at most 128 MiB of HBM per device.

v0:
```python
import jax
import jax.numpy as jnp
from jax import lax
from jax.sharding import PartitionSpec as P


def route_ranks(flat_routes):
    count = flat_routes.shape[0]
    same = flat_routes[:, None] == flat_routes[None, :]
    earlier = (
        jnp.arange(count, dtype=jnp.int32)[:, None] > jnp.arange(count, dtype=jnp.int32)[None, :]
    )
    return jnp.sum((same & earlier).astype(jnp.int32), axis=1)


def expert_backward(rows_in, grads_in, gate_w, up_w, down_w):
    gate_pre = jnp.dot(rows_in, gate_w, preferred_element_type=jnp.float32)
    up_pre = jnp.dot(rows_in, up_w, preferred_element_type=jnp.float32)
    gate_sig = jax.nn.sigmoid(gate_pre)
    gate_act = gate_pre * gate_sig
    hidden = (gate_act * up_pre).astype(jnp.bfloat16)
    expert_out = jnp.dot(hidden, down_w, preferred_element_type=jnp.float32)
    scores = jnp.sum(grads_in.astype(jnp.float32) * expert_out, axis=1)
    contract = (((1,), (1,)), ((), ()))
    hidden_grad = lax.dot_general(grads_in, down_w, contract, preferred_element_type=jnp.float32)
    up_grad = (hidden_grad * gate_act).astype(jnp.bfloat16)
    pre_grad = (hidden_grad * up_pre * gate_sig * (1.0 + gate_pre * (1.0 - gate_sig))).astype(
        jnp.bfloat16
    )
    returned = lax.dot_general(pre_grad, gate_w, contract, preferred_element_type=jnp.float32)
    returned = returned + lax.dot_general(
        up_grad, up_w, contract, preferred_element_type=jnp.float32
    )
    return (returned, scores)


def shards(tokens, out_grad, routes, gates, w_gate, w_up, w_down):
    node_count = lax.axis_size("node")
    local_count = lax.axis_size("local")
    experts = node_count * local_count
    tok_rows, route_count = routes.shape
    count = tok_rows * route_count
    slots = count // experts + 1
    width = experts * slots
    features = tokens.shape[1]
    flat_routes = routes.reshape(count)
    slot_of = flat_routes * slots + route_ranks(flat_routes)
    placing = jnp.arange(width, dtype=jnp.int32)[:, None] == slot_of[None, :]
    placing = jnp.any(placing.reshape(width, tok_rows, route_count), axis=2).astype(jnp.bfloat16)
    send_rows = jnp.dot(placing, tokens, preferred_element_type=jnp.float32).astype(jnp.bfloat16)
    send_grads = jnp.dot(placing, out_grad, preferred_element_type=jnp.float32).astype(jnp.bfloat16)
    gate_w = w_gate[0]
    up_w = w_up[0]
    down_w = w_down[0]
    rows_in = lax.all_to_all(
        send_rows.reshape(experts, slots, features),
        ("node", "local"),
        split_axis=0,
        concat_axis=0,
        tiled=True,
    )
    grads_in = lax.all_to_all(
        send_grads.reshape(experts, slots, features),
        ("node", "local"),
        split_axis=0,
        concat_axis=0,
        tiled=True,
    )
    senders = rows_in.shape[0]
    items = rows_in.shape[1]
    returned, scores = expert_backward(
        rows_in.reshape(senders * items, features),
        grads_in.reshape(senders * items, features),
        gate_w,
        up_w,
        down_w,
    )
    back_rows = lax.all_to_all(
        returned.reshape(senders, items, features),
        ("node", "local"),
        split_axis=0,
        concat_axis=0,
        tiled=True,
    )
    back_scores = lax.all_to_all(
        scores.reshape(senders, items), ("node", "local"), split_axis=0, concat_axis=0, tiled=True
    )
    back_rows = back_rows.reshape(width, features)
    back_scores = back_scores.reshape(width)
    picked = back_rows[slot_of].reshape(tok_rows, route_count, features)
    input_grad = jnp.sum(gates[:, :, None] * picked, axis=1).astype(jnp.bfloat16)
    gate_grad = back_scores[slot_of].reshape(tok_rows, route_count)
    return (input_grad, gate_grad)


def solution(mesh):
    return jax.shard_map(
        shards,
        mesh=mesh,
        in_specs=(
            P(("node", "local"), None),
            P(("node", "local"), None),
            P(("node", "local"), None),
            P(("node", "local"), None),
            P(("node", "local"), None, None),
            P(("node", "local"), None, None),
            P(("node", "local"), None, None),
        ),
        out_specs=(P(("node", "local"), None), P(("node", "local"), None)),
        check_vma=False,
    )
```

profile of v0, /device:TPU:1, one launch (start us, length us, event | category | flops | bytes accessed | tf_op | source)
XLA Modules:
  0.0 486.7 jit_solution(2738961161257274997)
XLA Ops:
  0.6 0.0 copy-start
  0.6 0.9 copy.31
  1.5 0.1 eq.30
  1.6 0.3 convert_reduce_fusion
  1.9 0.1 reduce_sum.32
  2.0 0.1 copy.33
  2.1 0.2 fusion.19
  2.3 0.0 copy-done
  2.3 3.0 convolution_convert_fusion
  5.2 6.2 %copy.35 = bf16[640,2880]{1,0:T(8,128)(2,1)} copy(bf16[640,2880]{0,1:T(8,128)(2,1)} %convolution_convert_fusion) | data formatting | bytes 7372800 | tf_op jit(solution)/shard_map/convert_element_type | solution.py:50
  11.4 7.3 %reshape.87 = bf16[128,5,2880]{2,1,0:T(8,128)(2,1)} reshape(bf16[640,2880]{1,0:T(8,128)(2,1)} %copy.35) | data formatting | bytes 7372800 | tf_op jit(solution)/shard_map/reshape | solution.py:56
  18.7 0.0 copy-start.4
  18.7 11.9 %all-to-all-start.1 = ((bf16[128,5,2880]{2,1,0:T(8,128)(2,1)}), bf16[128,5,2880]{2,1,0:T(8,128)(2,1)}, u32[]{:S(2)}, u32[]{:S(2)}) async-start(bf16[128,5,2880]{2,1,0:T(8,128)(2,1)} %reshape.87), calls=%async_computation.1 | async-start | bytes 12058624 | tf_op jit(solution)/shard_map/all_to_all | solution.py:55
  30.6 0.0 copy-done.4
  30.7 3.0 convolution_convert_fusion.1
  33.7 6.1 %copy.34 = bf16[640,2880]{1,0:T(8,128)(2,1)} copy(bf16[640,2880]{0,1:T(8,128)(2,1)} %convolution_convert_fusion.1) | data formatting | bytes 7372800 | tf_op jit(solution)/shard_map/convert_element_type | solution.py:51
  39.8 7.4 %reshape.85 = bf16[128,5,2880]{2,1,0:T(8,128)(2,1)} reshape(bf16[640,2880]{1,0:T(8,128)(2,1)} %copy.34) | data formatting | bytes 7372800 | tf_op jit(solution)/shard_map/reshape | solution.py:63
  47.2 56.3 %all-to-all-done.1 = bf16[128,5,2880]{2,1,0:T(8,128)(2,1)} async-done(((bf16[128,5,2880]{2,1,0:T(8,128)(2,1)}), bf16[128,5,2880]{2,1,0:T(8,128)(2,1)}, u32[]{:S(2)}, u32[]{:S(2)}) %all-to-all-start.1) | async-done | bytes 3686432 | tf_op jit(solution)/shard_map/all_to_all | solution.py:55
  103.5 8.4 %all-to-all-start = ((bf16[128,5,2880]{2,1,0:T(8,128)(2,1)}), bf16[128,5,2880]{2,1,0:T(8,128)(2,1)}, u32[]{:S(2)}, u32[]{:S(2)}) async-start(bf16[128,5,2880]{2,1,0:T(8,128)(2,1)} %reshape.85), calls=%async_computation | async-start | bytes 12058624 | tf_op jit(solution)/shard_map/all_to_all | solution.py:62
  111.9 8.0 %reshape.88 = bf16[640,2880]{1,0:T(8,128)(2,1)} reshape(bf16[128,5,2880]{2,1,0:T(8,128)(2,1)} %all-to-all-done.1) | data formatting | bytes 7372800 | tf_op jit(solution)/shard_map/reshape | solution.py:72
  119.8 0.0 copy-start.2
  119.8 12.9 %fusion.2 = f32[640,1440]{0,1:T(8,128)} fusion(bf16[640,2880]{1,0:T(8,128)(2,1)} %reshape.88, bf16[1,2880,1440]{1,2,0:T(8,128)(2,1)} %param.11), kind=kOutput, calls=%fused_computation.4 | convolution fusion | flops 5308416000 | bytes 15667200 | tf_op jit(solution)/shard_map/dot_general | solution.py:17
  132.8 0.0 copy-done.2
  132.8 10.7 %fusion.6 = f32[640,1440]{0,1:T(8,128)} fusion(bf16[640,2880]{1,0:T(8,128)(2,1)S(1)} %copy-done.2, bf16[1,2880,1440]{1,2,0:T(8,128)(2,1)} %param.12), kind=kOutput, calls=%fused_computation.8 | convolution fusion | flops 5308416000 | bytes 15667200 | tf_op jit(solution)/shard_map/dot_general | solution.py:18
  143.4 41.2 %all-to-all-done = bf16[128,5,2880]{2,1,0:T(8,128)(2,1)} async-done(((bf16[128,5,2880]{2,1,0:T(8,128)(2,1)}), bf16[128,5,2880]{2,1,0:T(8,128)(2,1)}, u32[]{:S(2)}, u32[]{:S(2)}) %all-to-all-start) | async-done | bytes 3686432 | tf_op jit(solution)/shard_map/all_to_all | solution.py:62
  184.7 8.0 %reshape.86 = bf16[640,2880]{1,0:T(8,128)(2,1)} reshape(bf16[128,5,2880]{2,1,0:T(8,128)(2,1)} %all-to-all-done) | data formatting | bytes 7372800 | tf_op jit(solution)/shard_map/reshape | solution.py:73
  192.7 6.0 %copy.37 = bf16[640,2880]{0,1:T(8,128)(2,1)} copy(bf16[640,2880]{1,0:T(8,128)(2,1)} %reshape.86) | data formatting | bytes 7372800 | tf_op jit(solution)/shard_map/reshape | solution.py:73
  198.6 0.0 copy-start.3
  198.6 0.0 copy-start.6
  198.6 0.0 copy-start.8
  198.6 12.0 %fusion.10 = f32[640,1440]{0,1:T(8,128)} fusion(bf16[640,2880]{1,0:T(8,128)(2,1)} %reshape.86, bf16[1,1440,2880]{2,1,0:T(8,128)(2,1)} %param.13), kind=kOutput, calls=%fused_computation.12 | convolution fusion | flops 5308416000 | bytes 15667200 | tf_op jit(solution)/shard_map/dot_general | solution.py:25
  210.7 0.0 copy-done.3
  210.7 0.0 copy-done.6
  210.7 0.0 copy-done.8
  210.7 10.8 %multiply_reduce_fusion = f32[640]{0:T(1024)S(1)} fusion(bf16[640,2880]{0,1:T(8,128)(2,1)S(1)} %copy-done.3, bf16[1,1440,2880]{2,1,0:T(8,128)(2,1)} %param.13, f32[640,1440]{0,1:T(8,128)S(1)} %copy-done.8, f32[640,1440]{0,1:T(8,128)S(1)} %copy-done.6), kind=kOutput, calls=%fused_computation.14 | convolution fusion | flops 5319474688 | bytes 19356160 | tf_op jit(solution)/shard_map/dot_general | solution.py:22
  221.5 0.8 all_to_all.18
  222.4 8.0 %all-to-all-start.3 = ((f32[128,1,5]{2,1,0:T(1,128)}), f32[128,1,5]{2,1,0:T(1,128)S(1)}, u32[]{:S(2)}, u32[]{:S(2)}) async-start(f32[128,1,5]{2,1,0:T(1,128)} %bitcast.5), calls=%async_computation.3 | async-start | bytes 131072 | tf_op jit(solution)/shard_map/all_to_all | solution.py:85
  230.4 0.0 copy-start.7
  230.4 21.1 %fusion = f32[640,2880]{0,1:T(8,128)S(1)} fusion(bf16[1,2880,1440]{1,2,0:T(8,128)(2,1)} %param.11, f32[640,1440]{0,1:T(8,128)} %fusion.2, f32[640,1440]{0,1:T(8,128)} %fusion.10, f32[640,1440]{0,1:T(8,128)} %fusion.6), kind=kOutput, calls=%fused_computation.2 | convolution fusion | flops 5317632000 | bytes 26726400 | tf_op jit(solution)/shard_map/dot_general | solution.py:30
  251.5 0.0 copy-done.7
  251.5 13.2 %fusion.14 = f32[640,2880]{0,1:T(8,128)} fusion(f32[640,2880]{0,1:T(8,128)S(1)} %fusion, bf16[1,2880,1440]{1,2,0:T(8,128)(2,1)} %param.12, f32[640,1440]{0,1:T(8,128)} %fusion.10, f32[640,1440]{0,1:T(8,128)S(1)} %copy-done.7), kind=kOutput, calls=%fused_computation.16 | convolution fusion | flops 5315788800 | bytes 30412800 | tf_op jit(solution)/shard_map/dot_general | solution.py:31
  264.7 8.9 %copy.36 = f32[640,2880]{1,0:T(8,128)} copy(f32[640,2880]{0,1:T(8,128)} %fusion.14) | data formatting | bytes 14745600 | tf_op jit(solution)/shard_map/add | solution.py:31
  273.6 9.4 %reshape.89 = f32[128,5,2880]{2,1,0:T(8,128)} reshape(f32[640,2880]{1,0:T(8,128)} %copy.36) | data formatting | bytes 14745600 | tf_op jit(solution)/shard_map/reshape | solution.py:79
  283.0 0.0 copy-start.5
  283.0 0.0 all-to-all-done.3
  283.0 10.2 %all-to-all-start.2 = ((f32[128,5,2880]{2,1,0:T(8,128)}), f32[128,5,2880]{2,1,0:T(8,128)}, u32[]{:S(2)}, u32[]{:S(2)}) async-start(f32[128,5,2880]{2,1,0:T(8,128)} %reshape.89), calls=%async_computation.2 | async-start | bytes 24117248 | tf_op jit(solution)/shard_map/all_to_all | solution.py:78
  293.2 0.1 mul.61
  293.3 0.0 copy-done.5
  293.3 0.1 copy.30
  293.4 0.5 broadcast.67
  293.9 0.8 reduce.3
  294.7 0.2 reshape.92
  294.9 2.3 gather_fusion.1
  297.2 0.1 reshape.93
  297.3 0.7 copy.40
  298.0 152.7 %all-to-all-done.2 = f32[128,5,2880]{2,1,0:T(8,128)} async-done(((f32[128,5,2880]{2,1,0:T(8,128)}), f32[128,5,2880]{2,1,0:T(8,128)}, u32[]{:S(2)}, u32[]{:S(2)}) %all-to-all-start.2) | async-done | bytes 7372832 | tf_op jit(solution)/shard_map/all_to_all | solution.py:78
  450.7 9.9 %reshape.90 = f32[640,2880]{1,0:T(8,128)} reshape(f32[128,5,2880]{2,1,0:T(8,128)} %all-to-all-done.2) | data formatting | bytes 14745600 | tf_op jit(solution)/shard_map/reshape | solution.py:88
  460.6 10.1 %gather_fusion = f32[512,2880]{1,0:T(8,128)} fusion(f32[640,2880]{1,0:T(8,128)} %reshape.90, s32[1024]{0:T(1024)S(1)} %pad_clamp_fusion), kind=kCustom, calls=%fused_computation | custom fusion | bytes 11798528 | tf_op jit(solution)/shard_map/gather | solution.py:90
  470.8 0.0 copy-start.1
  470.8 7.7 %reshape.91 = f32[128,4,2880]{2,1,0:T(4,128)} reshape(f32[512,2880]{1,0:T(8,128)} %gather_fusion) | data formatting | bytes 11796480 | tf_op jit(solution)/shard_map/reshape | solution.py:90
  478.4 7.1 %multiply_reduce_fusion.1 = bf16[128,2880]{1,0:T(8,128)(2,1)S(1)} fusion(f32[128,4,2880]{2,1,0:T(4,128)} %reshape.91, f32[128,4]{1,0:T(8,128)S(1)} %copy.30), kind=kLoop, calls=%fused_computation.15 | loop fusion | flops 2580480 | bytes 6637568 | tf_op jit(solution)/shard_map/reduce_sum | solution.py:91
  485.5 1.1 copy.39
  486.7 0.0 copy-done.1
  (3 shorter events, 0.0 us)
Async XLA Ops:
  0.6 1.6 copy-start
  18.7 11.9 %copy-start.4 = (bf16[128,2880]{0,1:T(8,128)(2,1)S(1)}, bf16[128,2880]{0,1:T(8,128)(2,1)}, u32[]{:S(2)}) copy-start(bf16[128,2880]{0,1:T(8,128)(2,1)} %param.8) | copy-start | bytes 2211844
  18.7 84.7 %all-to-all-start.1 = ((bf16[128,5,2880]{2,1,0:T(8,128)(2,1)}), bf16[128,5,2880]{2,1,0:T(8,128)(2,1)}, u32[]{:S(2)}, u32[]{:S(2)}) async-start(bf16[128,5,2880]{2,1,0:T(8,128)(2,1)} %reshape.87), calls=%async_computation.1 | async-start | bytes 12058624 | tf_op jit(solution)/shard_map/all_to_all | solution.py:55
  103.5 81.2 %all-to-all-start = ((bf16[128,5,2880]{2,1,0:T(8,128)(2,1)}), bf16[128,5,2880]{2,1,0:T(8,128)(2,1)}, u32[]{:S(2)}, u32[]{:S(2)}) async-start(bf16[128,5,2880]{2,1,0:T(8,128)(2,1)} %reshape.85), calls=%async_computation | async-start | bytes 12058624 | tf_op jit(solution)/shard_map/all_to_all | solution.py:62
  119.8 12.9 %copy-start.2 = (bf16[640,2880]{1,0:T(8,128)(2,1)S(1)}, bf16[640,2880]{1,0:T(8,128)(2,1)}, u32[]{:S(2)}) copy-start(bf16[640,2880]{1,0:T(8,128)(2,1)} %reshape.88) | copy-start | bytes 11059204
  198.6 12.0 %copy-start.3 = (bf16[640,2880]{0,1:T(8,128)(2,1)S(1)}, bf16[640,2880]{0,1:T(8,128)(2,1)}, u32[]{:S(2)}) copy-start(bf16[640,2880]{0,1:T(8,128)(2,1)} %copy.37) | copy-start | bytes 11059204
  198.6 12.0 %copy-start.6 = (f32[640,1440]{0,1:T(8,128)S(1)}, f32[640,1440]{0,1:T(8,128)}, u32[]{:S(2)}) copy-start(f32[640,1440]{0,1:T(8,128)} %fusion.2) | copy-start | bytes 11059204
  198.6 12.0 %copy-start.8 = (f32[640,1440]{0,1:T(8,128)S(1)}, f32[640,1440]{0,1:T(8,128)}, u32[]{:S(2)}) copy-start(f32[640,1440]{0,1:T(8,128)} %fusion.6) | copy-start | bytes 11059204
  222.4 60.6 %all-to-all-start.3 = ((f32[128,1,5]{2,1,0:T(1,128)}), f32[128,1,5]{2,1,0:T(1,128)S(1)}, u32[]{:S(2)}, u32[]{:S(2)}) async-start(f32[128,1,5]{2,1,0:T(1,128)} %bitcast.5), calls=%async_computation.3 | async-start | bytes 131072 | tf_op jit(solution)/shard_map/all_to_all | solution.py:85
  230.4 21.1 %copy-start.7 = (f32[640,1440]{0,1:T(8,128)S(1)}, f32[640,1440]{0,1:T(8,128)}, u32[]{:S(2)}) copy-start(f32[640,1440]{0,1:T(8,128)} %fusion.2) | copy-start | bytes 11059204
  283.0 10.3 %copy-start.5 = (f32[128,4]{0,1:T(4,128)S(1)}, f32[128,4]{0,1:T(4,128)}, u32[]{:S(2)}) copy-start(f32[128,4]{0,1:T(4,128)} %param.10) | copy-start | bytes 6148
  283.0 167.8 %all-to-all-start.2 = ((f32[128,5,2880]{2,1,0:T(8,128)}), f32[128,5,2880]{2,1,0:T(8,128)}, u32[]{:S(2)}, u32[]{:S(2)}) async-start(f32[128,5,2880]{2,1,0:T(8,128)} %reshape.89), calls=%async_computation.2 | async-start | bytes 24117248 | tf_op jit(solution)/shard_map/all_to_all | solution.py:78
  470.8 15.9 %copy-start.1 = (bf16[128,2880]{0,1:T(8,128)(2,1)S(1)}, bf16[128,2880]{0,1:T(8,128)(2,1)}, u32[]{:S(2)}) copy-start(bf16[128,2880]{0,1:T(8,128)(2,1)} %param.7) | copy-start | bytes 2211844
where the time goes:
time: 489 us; the launch traced here: 487 us
  waiting for transfers between devices  250 us (51%)
  local copies, waits for them, and re-layouts  102 us (21%)
  matrix products  86.7 us (18%)
  starting transfers between devices  38.5 us (8%)
  other arithmetic  8.33 us (2%)
    all_to_all x1, waiting for transfers between devices, shards(): lax.all_to_all(returned.reshape(senders, items, features), ('node', 'loca...  153 us
    all_to_all x1, waiting for transfers between devices, shards(): lax.all_to_all(send_rows.reshape(experts, slots, features), ('node', 'loc...  56.3 us
    all_to_all x1, waiting for transfers between devices, shards(): lax.all_to_all(send_grads.reshape(experts, slots, features), ('node', 'lo...  41.2 us
    dot_general x1, matrix products, expert_backward(): lax.dot_general(pre_grad, gate_w, contract, preferred_element_type=jnp.fl...  21.1 us
    reshape x2, local copies, waits for them, and re-layouts, shards(): grads_in.reshape(senders * items, features)  14 us
    dot_general x1, matrix products, expert_backward(): lax.dot_general(up_grad, up_w, contract, preferred_element_type=jnp.float32)  13.2 us
    dot_general x1, matrix products, expert_backward(): gate_pre = jnp.dot(rows_in, gate_w, preferred_element_type=jnp.float32)  12.9 us
    dot_general x1, matrix products, expert_backward(): lax.dot_general(grads_in, down_w, contract, preferred_element_type=jnp.fl...  12 us
  transfers between devices with their start and end apart: 4, of which 3 were waited for; matrix products, arithmetic and copies ran while one was open for 22% of the time, Pallas kernels for 0%

commit v1 on v0

v1 whole, which is shorter than its diff:
```python
import functools

import jax
import jax.numpy as jnp
from jax import lax
from jax.experimental import pallas as pl
from jax.experimental.pallas import tpu as pltpu
from jax.sharding import PartitionSpec as P

LANES = 128
GROUP = 16
SLOTS = 5
BF = jnp.bfloat16
F32 = jnp.float32
NT = (((1,), (1,)), ((), ()))
VMEM_LIMIT = 60 * 1024 * 1024


def round_up(value, step):
    return -(-value // step) * step


def route_maps(routes_t):
    topk, tokens = routes_t.shape
    expert = lax.broadcasted_iota(jnp.int32, (LANES, tokens), 0)
    named = [jnp.where(routes_t[k : k + 1, :] == expert, 1.0, 0.0) for k in range(topk)]
    total = functools.reduce(lambda a, b: a + b, named)
    row = lax.broadcasted_iota(jnp.int32, (tokens, tokens), 0)
    column = lax.broadcasted_iota(jnp.int32, (tokens, tokens), 1)
    earlier = jnp.where(row < column, 1.0, 0.0).astype(BF)
    rank = jnp.dot(total.astype(BF), earlier, preferred_element_type=F32)
    return named, total, rank


def pack_rows(step, load, stage_ref, out_ref, tensors, tiles, pitch):
    base = pl.multiple_of(step * GROUP, GROUP)
    for j in range(tensors):
        for s in range(SLOTS):
            for t in range(tiles):
                value = load(j, pl.ds(s * LANES + base, GROUP), slice(t * LANES, (t + 1) * LANES))
                stage_ref[pl.ds((j * SLOTS + s) * tiles + t, GROUP, stride=pitch), :] = value.astype(F32)
    rows = out_ref.shape[1]
    for a in range(GROUP):
        out_ref[a] = stage_ref[a * pitch : a * pitch + rows, :].astype(BF)


def unpack_rows(step, in_ref, stage_ref, store, tensors, tiles, pitch):
    base = pl.multiple_of(step * GROUP, GROUP)
    rows = in_ref.shape[1]
    for a in range(GROUP):
        stage_ref[a * pitch : a * pitch + rows, :] = in_ref[a].astype(F32)
    for j in range(tensors):
        for s in range(SLOTS):
            for t in range(tiles):
                value = stage_ref[pl.ds((j * SLOTS + s) * tiles + t, GROUP, stride=pitch), :]
                store(j, pl.ds(s * LANES + base, GROUP), slice(t * LANES, (t + 1) * LANES), value.astype(BF))


def dispatch_kernel(tiles, pitch, routes_ref, tok_ref, grad_ref, out_ref, rows_ref, stage_ref):
    step = pl.program_id(0)
    features = tok_ref.shape[0]

    @pl.when(step == 0)
    def _():
        stage_ref[...] = jnp.zeros_like(stage_ref)
        rows_ref[:, :, (tiles - 1) * LANES :] = jnp.zeros((2, SLOTS * LANES, LANES), BF)
        _, total, rank = route_maps(routes_ref[...])
        place = jnp.concatenate(
            [jnp.where(rank == float(s), total, 0.0).astype(BF) for s in range(SLOTS)], axis=0
        )
        for j, ref in enumerate((tok_ref, grad_ref)):
            for lo in range(0, features, 512):
                hi = min(lo + 512, features)
                part = lax.dot_general(place, ref[lo:hi, :], NT, preferred_element_type=F32)
                rows_ref[j, :, lo:hi] = part.astype(BF)

    pack_rows(step, lambda j, r, c: rows_ref[j, r, c], stage_ref, out_ref, 2, tiles, pitch)


def dispatch(routes_t, tok_t, grad_t):
    features, tokens = tok_t.shape
    tiles = -(-features // LANES)
    rows = round_up(2 * SLOTS * tiles, 8)
    pitch = rows + 1
    return pl.pallas_call(
        functools.partial(dispatch_kernel, tiles, pitch),
        grid=(LANES // GROUP,),
        in_specs=[
            pl.BlockSpec(routes_t.shape, lambda i: (0, 0)),
            pl.BlockSpec(tok_t.shape, lambda i: (0, 0)),
            pl.BlockSpec(grad_t.shape, lambda i: (0, 0)),
        ],
        out_specs=pl.BlockSpec((GROUP, rows, LANES), lambda i: (i, 0, 0)),
        out_shape=jax.ShapeDtypeStruct((LANES, rows, LANES), BF),
        scratch_shapes=[
            pltpu.VMEM((2, SLOTS * LANES, tiles * LANES), BF),
            pltpu.VMEM((GROUP * pitch, LANES), F32),
        ],
        compiler_params=pltpu.CompilerParams(vmem_limit_bytes=VMEM_LIMIT),
    )(routes_t, tok_t, grad_t)


def expert_kernel(
    tiles, pitch_in, pitch_out, in_ref, gate_hbm, up_hbm, down_hbm, out_ref,
    rows_ref, back_ref, pre_ref, upg_ref, gate_ref, up_ref, down_ref, stage_ref, stage_out_ref, sems,
):
    step = pl.program_id(0)
    steps = LANES // GROUP
    hidden, features = gate_hbm.shape
    copies = [
        pltpu.make_async_copy(src, dst, sems.at[i])
        for i, (src, dst) in enumerate(((gate_hbm, gate_ref), (up_hbm, up_ref), (down_hbm, down_ref)))
    ]

    @pl.when(step == 0)
    def _():
        for copy in copies:
            copy.start()

    @pl.when(step < steps)
    def _():
        def store(j, r, c, value):
            rows_ref[j, r, c] = value

        unpack_rows(step, in_ref, stage_ref, store, 2, tiles, pitch_in)

    @pl.when(step == steps - 1)
    def _():
        stage_out_ref[...] = jnp.zeros_like(stage_out_ref)
        for copy in copies:
            copy.wait()
        tok = rows_ref.at[0]
        grad = rows_ref.at[1]
        score = jnp.zeros((SLOTS * LANES, 1), F32)
        for lo in range(0, hidden, 512):
            hi = min(lo + 512, hidden)
            x = tok[:, :features]
            gate_pre = lax.dot_general(x, gate_ref[lo:hi, :], NT, preferred_element_type=F32)
            up_pre = lax.dot_general(x, up_ref[lo:hi, :], NT, preferred_element_type=F32)
            hidden_grad = lax.dot_general(
                grad[:, :features], down_ref[lo:hi, :], NT, preferred_element_type=F32
            )
            sig = jax.nn.sigmoid(gate_pre)
            act = gate_pre * sig
            act_up = (act * up_pre).astype(BF).astype(F32)
            score = score + jnp.sum(act_up * hidden_grad, axis=1, keepdims=True)
            upg_ref[:, lo:hi] = (hidden_grad * act).astype(BF)
            pre_ref[:, lo:hi] = (hidden_grad * up_pre * sig * (1.0 + gate_pre * (1.0 - sig))).astype(BF)
        high = score.astype(BF)
        low = (score - high.astype(F32)).astype(BF)
        whole = features // 256

        def columns(lo, width):
            back = jnp.dot(pre_ref[...], gate_ref[:, pl.ds(lo, width)], preferred_element_type=F32)
            return back + jnp.dot(upg_ref[...], up_ref[:, pl.ds(lo, width)], preferred_element_type=F32)

        @pl.loop(0, whole)
        def _(n):
            lo = pl.multiple_of(n * 256, 256)
            back_ref[:, pl.ds(lo, 256)] = columns(lo, 256).astype(BF)

        rest = features - whole * 256
        lane = lax.broadcasted_iota(jnp.int32, (SLOTS * LANES, LANES), 1)
        last = jnp.where(lane == rest, high.astype(F32), jnp.where(lane == rest + 1, low.astype(F32), 0.0))
        back_ref[:, whole * 256 :] = last.astype(BF)
        back_ref[:, whole * 256 : features] = columns(whole * 256, rest).astype(BF)

    @pl.when(step >= steps)
    def _():
        pack_rows(step - steps, lambda j, r, c: back_ref[r, c], stage_out_ref, out_ref, 1, tiles, pitch_out)


def expert(recv, gate_t, up_t, down):
    peers, rows_in, _ = recv.shape
    hidden, features = gate_t.shape
    tiles = -(-features // LANES)
    rows_out = round_up(SLOTS * tiles, 8)
    steps = LANES // GROUP
    pitch_in, pitch_out = rows_in + 1, rows_out + 1
    wide = SLOTS * LANES
    flops = 5 * 2 * wide * hidden * features
    return pl.pallas_call(
        functools.partial(expert_kernel, tiles, pitch_in, pitch_out),
        grid=(2 * steps,),
        in_specs=[
            pl.BlockSpec((GROUP, rows_in, LANES), lambda i: (jnp.minimum(i, steps - 1), 0, 0)),
            pl.BlockSpec(memory_space=pl.ANY),
            pl.BlockSpec(memory_space=pl.ANY),
            pl.BlockSpec(memory_space=pl.ANY),
        ],
        out_specs=pl.BlockSpec((GROUP, rows_out, LANES), lambda i: (jnp.maximum(i - steps, 0), 0, 0)),
        out_shape=jax.ShapeDtypeStruct((peers, rows_out, LANES), BF),
        scratch_shapes=[
            pltpu.VMEM((2, wide, tiles * LANES), BF),
            pltpu.VMEM((wide, tiles * LANES), BF),
            pltpu.VMEM((wide, hidden), BF),
            pltpu.VMEM((wide, hidden), BF),
            pltpu.VMEM((hidden, features), BF),
            pltpu.VMEM((hidden, features), BF),
            pltpu.VMEM((hidden, features), BF),
            pltpu.VMEM((GROUP * pitch_in, LANES), F32),
            pltpu.VMEM((GROUP * pitch_out, LANES), F32),
            pltpu.SemaphoreType.DMA((3,)),
        ],
        compiler_params=pltpu.CompilerParams(vmem_limit_bytes=VMEM_LIMIT),
        cost_estimate=pl.CostEstimate(flops=flops, bytes_accessed=40_000_000, transcendentals=0),
    )(recv, gate_t, up_t, down)


def combine_kernel(tiles, pitch, routes_ref, gates_ref, in_ref, out_ref, score_ref, rows_ref, stage_ref):
    step = pl.program_id(0)
    features, tokens = out_ref.shape

    def store(j, r, c, value):
        rows_ref[r, c] = value

    unpack_rows(step, in_ref, stage_ref, store, 1, tiles, pitch)

    @pl.when(step == LANES // GROUP - 1)
    def _():
        named, _, rank = route_maps(routes_ref[...])
        gates = gates_ref[...]
        weight = functools.reduce(lambda a, b: a + b, [m * gates[k : k + 1, :] for k, m in enumerate(named)])
        mixed = jnp.concatenate([jnp.where(rank == float(s), weight, 0.0).T for s in range(SLOTS)], axis=1)
        high = mixed.astype(BF)
        low = (mixed - high.astype(F32)).astype(BF)
        both = jnp.concatenate([high, low], axis=0)
        for lo in range(0, features, 512):
            hi = min(lo + 512, features)
            part = jnp.dot(both, rows_ref[:, lo:hi], preferred_element_type=F32)
            part = part[:tokens] + part[tokens:]
            out_ref[lo:hi, :] = part.T.astype(BF)
        rest = features - (tiles - 1) * LANES
        last = rows_ref[:, (tiles - 1) * LANES :].astype(F32)
        score = last[:, rest : rest + 1] + last[:, rest + 1 : rest + 2]
        for k, m in enumerate(named):
            terms = [
                jnp.where(rank == float(s), m, 0.0) * score[s * LANES : (s + 1) * LANES]
                for s in range(SLOTS)
            ]
            score_ref[k : k + 1, :] = jnp.sum(
                functools.reduce(lambda a, b: a + b, terms), axis=0, keepdims=True
            )


def combine(routes_t, gates_t, recv, features):
    topk, tokens = routes_t.shape
    tiles = -(-features // LANES)
    rows = recv.shape[1]
    pitch = rows + 1
    return pl.pallas_call(
        functools.partial(combine_kernel, tiles, pitch),
        grid=(LANES // GROUP,),
        in_specs=[
            pl.BlockSpec(routes_t.shape, lambda i: (0, 0)),
            pl.BlockSpec(gates_t.shape, lambda i: (0, 0)),
            pl.BlockSpec((GROUP, rows, LANES), lambda i: (i, 0, 0)),
        ],
        out_specs=[
            pl.BlockSpec((features, tokens), lambda i: (0, 0)),
            pl.BlockSpec((topk, tokens), lambda i: (0, 0)),
        ],
        out_shape=[
            jax.ShapeDtypeStruct((features, tokens), BF),
            jax.ShapeDtypeStruct((topk, tokens), F32),
        ],
        scratch_shapes=[
            pltpu.VMEM((SLOTS * LANES, tiles * LANES), BF),
            pltpu.VMEM((GROUP * pitch, LANES), F32),
        ],
        compiler_params=pltpu.CompilerParams(vmem_limit_bytes=VMEM_LIMIT),
    )(routes_t, gates_t, recv)


def exchange(messages):
    return lax.all_to_all(messages, ("node", "local"), split_axis=0, concat_axis=0, tiled=True)


def shards(tokens, out_grad, routes, gates, w_gate, w_up, w_down):
    features = tokens.shape[1]
    routes_t, gates_t = routes.T, gates.T
    gate_t = jnp.swapaxes(w_gate, 1, 2)[0]
    up_t = jnp.swapaxes(w_up, 1, 2)[0]
    recv = exchange(dispatch(routes_t, tokens.T, out_grad.T))
    back = exchange(expert(recv, gate_t, up_t, w_down[0]))
    input_grad_t, gate_grad_t = combine(routes_t, gates_t, back, features)
    return (input_grad_t.T, gate_grad_t.T)


def solution(mesh):
    both = ("node", "local")
    return jax.shard_map(
        shards,
        mesh=mesh,
        in_specs=(P(both, None),) * 4 + (P(both, None, None),) * 3,
        out_specs=(P(both, None), P(both, None)),
        check_vma=False,
    )
```

time: 489 us -> 226 us (0.46)
  waiting for transfers between devices: 250 us -> 0 us
  blocking collectives: 0 us -> 157 us
  local copies, waits for them, and re-layouts: 102 us -> 0 us
  matrix products: 86.7 us -> 0 us
  Pallas kernels: 0 us -> 67.5 us
  starting transfers between devices: 38.5 us -> 0 us
  other arithmetic: 8.33 us -> 0 us
    all_to_all x4 -> x0, waiting for transfers between devices: 250 us -> none  [the longest x1 153 us: shards(): lax.all_to_all(returned.reshape(senders, items, features), ('node', 'loca...]
    all_to_all x0 -> x2, blocking collectives: none -> 157 us  [exchange(): lax.all_to_all(messages, ('node', 'local'), split_axis=0, concat_axis=0,...]
    dot_general x8 -> x0, matrix products: 86.7 us -> none  [the longest x1 21.1 us: expert_backward(): lax.dot_general(pre_grad, gate_w, contract, preferred_element_type=jnp.fl...]
    pallas_call x0 -> x3, Pallas kernels: none -> 67.5 us  [the longest x1 51.1 us: expert(): pl.pallas_call(functools.partial(expert_kernel, tiles, pitch_in, pitch_ou...]
    reshape x10 -> x0, local copies, waits for them, and re-layouts: 63.9 us -> none  [the longest x2 14 us: shards(): grads_in.reshape(senders * items, features)]
    all_to_all x4 -> x0, starting transfers between devices: 38.5 us -> none  [the longest x1 11.9 us: shards(): lax.all_to_all(send_rows.reshape(experts, slots, features), ('node', 'loc...]
    gather x2 -> x0, local copies, waits for them, and re-layouts: 12.4 us -> none  [the longest x1 10.1 us: shards(): picked = back_rows[slot_of].reshape(tok_rows, route_count, features)]
    convert_element_type x2 -> x0, local copies, waits for them, and re-layouts: 12.3 us -> none  [the longest x1 6.17 us: shards(): jnp.dot(placing, tokens, preferred_element_type=jnp.float32)]
  transfers between devices with their start and end apart: 4 -> 0, of which waited for: 3 -> 0; matrix products, arithmetic and copies ran while one was open for 22% -> 0% of each run, Pallas kernels for 0% -> 0%
where the time goes in v1:
time: 226 us; the launch traced here: 225 us
  blocking collectives  157 us (69%)
  Pallas kernels  67.5 us (30%)
    all_to_all x2, blocking collectives, exchange(): lax.all_to_all(messages, ('node', 'local'), split_axis=0, concat_axis=0,...  157 us
    pallas_call x1, Pallas kernels, expert(): pl.pallas_call(functools.partial(expert_kernel, tiles, pitch_in, pitch_ou...  51.1 us
    pallas_call x1, Pallas kernels, dispatch(): pl.pallas_call(functools.partial(dispatch_kernel, tiles, pitch), grid=(LA...  8.79 us
    pallas_call x1, Pallas kernels, combine(): pl.pallas_call(functools.partial(combine_kernel, tiles, pitch), grid=(LAN...  7.65 us

profile of v1, /device:TPU:1, one launch (start us, length us, event | category | flops | bytes accessed | tf_op | source)
XLA Modules:
  0.0 225.5 jit_solution(12015812497204341668)
XLA Ops:
  0.6 8.8 %shard_map.86 = bf16[128,232,128]{2,1,0:T(8,128)(2,1)} custom-call(s32[4,128]{1,0:T(4,128)} %bitcast.15, bf16[2880,128]{1,0:T(8,128)(2,1)} %bitcast.13, bf16[2880,128]{1,0:T(8,128)(2,1)} %bitcast.14), custom_call_target="tpu_custom_call" | custom-call | tf_op jit(solution)/shard_map/pallas_call | solution.py:85
  9.4 101.1 %all_to_all.10.in_ref = bf16[128,232,128]{2,1,0:T(8,128)(2,1)} all-to-all(bf16[128,232,128]{2,1,0:T(8,128)(2,1)} %shard_map.86), channel_id=1, replica_groups=mesh['node'=16,'local'=8] {'node','local'}, dimensions={0} | all-to-all | bytes 15204352 | tf_op jit(solution)/shard_map/all_to_all | solution.py:276
  110.6 51.1 %shard_map.87 = bf16[128,120,128]{2,1,0:T(8,128)(2,1)} custom-call(bf16[128,232,128]{2,1,0:T(8,128)(2,1)} %all_to_all.10.in_ref, bf16[1440,2880]{1,0:T(8,128)(2,1)} %bitcast.18, bf16[1440,2880]{1,0:T(8,128)(2,1)} %bitcast.19, bf16[1440,2880]{1,0:T(8,128)(2,1)} %bitcast.20), custom_call_target="tpu_custom_call" | custom-call | flops 26542080000 | bytes 40000000 | tf_op jit(solution)/shard_map/pallas_call | solution.py:182
  161.6 56.2 %all_to_all.11.in_ref = bf16[128,120,128]{2,1,0:T(8,128)(2,1)} all-to-all(bf16[128,120,128]{2,1,0:T(8,128)(2,1)} %shard_map.87), channel_id=1, replica_groups=mesh['node'=16,'local'=8] {'node','local'}, dimensions={0} | all-to-all | bytes 7864320 | tf_op jit(solution)/shard_map/all_to_all | solution.py:276
  217.8 7.7 %shard_map.88 = (bf16[2880,128]{1,0:T(8,128)(2,1)}, f32[4,128]{1,0:T(4,128)}) custom-call(s32[4,128]{1,0:T(4,128)} %bitcast.16, f32[4,128]{1,0:T(4,128)} %bitcast.17, bf16[128,120,128]{2,1,0:T(8,128)(2,1)} %all_to_all.11.in_ref), custom_call_target="tpu_custom_call" | custom-call | tf_op jit(solution)/shard_map/pallas_call | solution.py:251

commit v2 on v1

v2 whole, which is shorter than its diff:
```python
import functools

import jax
import jax.numpy as jnp
from jax import lax
from jax.experimental import pallas as pl
from jax.experimental.pallas import tpu as pltpu
from jax.sharding import PartitionSpec as P

LANES = 128
GROUP = 16
SLOTS = 5
PARTS = 4
BF = jnp.bfloat16
F32 = jnp.float32
NT = (((1,), (1,)), ((), ()))
VMEM_LIMIT = 60 * 1024 * 1024


def round_up(value, step):
    return -(-value // step) * step


def route_maps(routes_t):
    topk, tokens = routes_t.shape
    expert = lax.broadcasted_iota(jnp.int32, (LANES, tokens), 0)
    named = [jnp.where(routes_t[k : k + 1, :] == expert, 1.0, 0.0) for k in range(topk)]
    total = functools.reduce(lambda a, b: a + b, named)
    row = lax.broadcasted_iota(jnp.int32, (tokens, tokens), 0)
    column = lax.broadcasted_iota(jnp.int32, (tokens, tokens), 1)
    earlier = jnp.where(row < column, 1.0, 0.0).astype(BF)
    rank = jnp.dot(total.astype(BF), earlier, preferred_element_type=F32)
    return named, total, rank


def pack_messages(stage_ref, buffer_ref, rows, pitch, begin, end, finish):
    for first in range(begin, end, GROUP):
        for a in range(first, first + GROUP):
            buffer_ref[a, :rows] = stage_ref[a * pitch : a * pitch + rows, :].astype(BF)
        finish(first // GROUP)


def group_copies(source, target, sems):
    return [
        pltpu.make_async_copy(source(pl.ds(g * GROUP, GROUP)), target(pl.ds(g * GROUP, GROUP)), sems.at[g])
        for g in range(LANES // GROUP)
    ]


def dispatch_kernel(tiles, pitch, routes_ref, tok_ref, grad_ref, out_hbm, stage_ref, buffer_ref, sems):
    features = tok_ref.shape[0]
    peers, rows, _ = out_hbm.shape
    copies = group_copies(lambda g: buffer_ref.at[g], lambda g: out_hbm.at[g], sems)
    _, total, rank = route_maps(routes_ref[...])
    place = [jnp.where(rank == float(s), total, 0.0).astype(BF) for s in range(SLOTS)]

    def part_of(begin):
        count = peers // PARTS
        rows_of = jnp.concatenate([p[begin : begin + count] for p in place], axis=0)
        for j, ref in enumerate((tok_ref, grad_ref)):
            for lo in range(0, features, 256):
                hi = min(lo + 256, features)
                part = lax.dot_general(rows_of, ref[lo:hi, :], NT, preferred_element_type=F32)
                if (hi - lo) % LANES:
                    part = jnp.concatenate(
                        [part, jnp.zeros((part.shape[0], LANES - (hi - lo) % LANES), F32)], axis=1
                    )
                for s in range(SLOTS):
                    for t in range(part.shape[1] // LANES):
                        row = begin * pitch + (j * SLOTS + s) * tiles + lo // LANES + t
                        stage_ref[pl.ds(row, count, stride=pitch), :] = part[
                            s * count : (s + 1) * count, t * LANES : (t + 1) * LANES
                        ]

    for row in range(2 * SLOTS * tiles, rows):
        stage_ref[pl.ds(row, peers, stride=pitch), :] = jnp.zeros((peers, LANES), F32)
    for begin in range(0, peers, peers // PARTS):
        part_of(begin)
        pack_messages(
            stage_ref, buffer_ref, rows, pitch, begin, begin + peers // PARTS, lambda g: copies[g].start()
        )
    for copy in copies:
        copy.wait()


def dispatch(routes_t, tok_t, grad_t):
    features, tokens = tok_t.shape
    tiles = -(-features // LANES)
    rows = round_up(2 * SLOTS * tiles, 8)
    pitch = rows + 1
    return pl.pallas_call(
        functools.partial(dispatch_kernel, tiles, pitch),
        in_specs=[pl.BlockSpec(memory_space=pltpu.VMEM)] * 3,
        out_specs=pl.BlockSpec(memory_space=pl.ANY),
        out_shape=jax.ShapeDtypeStruct((LANES, rows, LANES), BF),
        scratch_shapes=[
            pltpu.VMEM((LANES * pitch, LANES), F32),
            pltpu.VMEM((LANES, rows, LANES), BF),
            pltpu.SemaphoreType.DMA((LANES // GROUP,)),
        ],
        compiler_params=pltpu.CompilerParams(vmem_limit_bytes=VMEM_LIMIT),
    )(routes_t, tok_t, grad_t)


def hidden_chunks(hidden):
    edges = [0, *range(256, hidden, 512), hidden]
    return list(zip(edges[:-1], edges[1:]))


def expert_kernel(
    tiles, pitch_in, pitch_out, in_hbm, gate_hbm, up_hbm, down_hbm, out_hbm,
    buffer_ref, rows_ref, pre_ref, upg_ref, gate_ref, up_ref, down_ref, stage_ref, in_sems, out_sems, w_sems,
):
    peers, rows_in, _ = in_hbm.shape
    rows_out = out_hbm.shape[1]
    hidden, features = gate_hbm.shape
    wide = SLOTS * peers
    arrivals = group_copies(lambda g: in_hbm.at[g], lambda g: buffer_ref.at[g], in_sems)
    departures = group_copies(
        lambda g: buffer_ref.at[g, pl.ds(0, rows_out)], lambda g: out_hbm.at[g], out_sems
    )
    chunks = hidden_chunks(hidden)
    weights = [
        [
            pltpu.make_async_copy(src.at[pl.ds(lo, hi - lo)], dst.at[pl.ds(lo, hi - lo)], w_sems.at[i, c])
            for i, (src, dst) in enumerate(((gate_hbm, gate_ref), (up_hbm, up_ref), (down_hbm, down_ref)))
        ]
        for c, (lo, hi) in enumerate(chunks)
    ]
    for copy in [*arrivals, *weights[0]]:
        copy.start()

    first_row = [0, (SLOTS * tiles) // 16 * 16]

    def unpack(j, g):
        start, count = first_row[j], rows_in - first_row[1]
        base = g * GROUP * pitch_out
        for a in range(GROUP):
            stage_ref[base + a * pitch_out : base + a * pitch_out + count, :] = buffer_ref[
                g * GROUP + a, start : start + count
            ].astype(F32)
        for s in range(SLOTS):
            for t in range(tiles):
                row = base + (j * SLOTS + s) * tiles + t - start
                value = stage_ref[pl.ds(row, GROUP, stride=pitch_out), :]
                first = s * peers + g * GROUP
                rows_ref[j, first : first + GROUP, t * LANES : (t + 1) * LANES] = value.astype(BF)

    for g, copy in enumerate(arrivals):
        copy.wait()
        unpack(0, g)

    score = jnp.zeros((wide, 1), F32)
    for c, (lo, hi) in enumerate(chunks):
        for copy in weights[c]:
            copy.wait()
        for copy in weights[c + 1] if c + 1 < len(chunks) else []:
            copy.start()
        x = rows_ref[0, :, :features]
        gate_pre = lax.dot_general(x, gate_ref[lo:hi, :], NT, preferred_element_type=F32)
        up_pre = lax.dot_general(x, up_ref[lo:hi, :], NT, preferred_element_type=F32)
        if c == 0:
            for g in range(len(arrivals)):
                unpack(1, g)
        hidden_grad = lax.dot_general(
            rows_ref[1, :, :features], down_ref[lo:hi, :], NT, preferred_element_type=F32
        )
        sig = jax.nn.sigmoid(gate_pre)
        act = gate_pre * sig
        act_up = (act * up_pre).astype(BF).astype(F32)
        score = score + jnp.sum(act_up * hidden_grad, axis=1, keepdims=True)
        upg_ref[:, lo:hi] = (hidden_grad * act).astype(BF)
        pre_ref[:, lo:hi] = (hidden_grad * up_pre * sig * (1.0 + gate_pre * (1.0 - sig))).astype(BF)
    high = score.astype(BF).astype(F32)
    low = score - high

    def place(value, row):
        for s in range(SLOTS):
            stage_ref[pl.ds(s * tiles + row, peers, stride=pitch_out), :] = value[
                s * peers : (s + 1) * peers
            ]

    def columns(lo, width):
        back = jnp.dot(pre_ref[...], gate_ref[:, pl.ds(lo, width)], preferred_element_type=F32)
        return back + jnp.dot(upg_ref[...], up_ref[:, pl.ds(lo, width)], preferred_element_type=F32)

    for row in range(SLOTS * tiles, rows_out):
        stage_ref[pl.ds(row, peers, stride=pitch_out), :] = jnp.zeros((peers, LANES), F32)
    whole = features // 256

    for n in range(whole):
        part = columns(n * 256, 256)
        place(part[:, :LANES], 2 * n)
        place(part[:, LANES:], 2 * n + 1)

    rest = features - whole * 256
    lane = lax.broadcasted_iota(jnp.int32, (wide, LANES - rest), 1)
    scores = jnp.where(lane == 0, high, jnp.where(lane == 1, low, 0.0))
    place(jnp.concatenate([columns(whole * 256, rest), scores], axis=1), 2 * whole)
    pack_messages(stage_ref, buffer_ref, rows_out, pitch_out, 0, peers, lambda g: departures[g].start())
    for copy in departures:
        copy.wait()


def expert(recv, gate_t, up_t, down):
    peers, rows_in, _ = recv.shape
    hidden, features = gate_t.shape
    tiles = -(-features // LANES)
    rows_out = round_up(SLOTS * tiles, 8)
    groups = LANES // GROUP
    pitch_in, pitch_out = rows_in + 1, rows_out + 1
    wide = SLOTS * LANES
    flops = 5 * 2 * wide * hidden * features
    return pl.pallas_call(
        functools.partial(expert_kernel, tiles, pitch_in, pitch_out),
        in_specs=[pl.BlockSpec(memory_space=pl.ANY)] * 4,
        out_specs=pl.BlockSpec(memory_space=pl.ANY),
        out_shape=jax.ShapeDtypeStruct((peers, rows_out, LANES), BF),
        scratch_shapes=[
            pltpu.VMEM((peers, rows_in, LANES), BF),
            pltpu.VMEM((2, wide, tiles * LANES), BF),
            pltpu.VMEM((wide, hidden), BF),
            pltpu.VMEM((wide, hidden), BF),
            pltpu.VMEM((hidden, features), BF),
            pltpu.VMEM((hidden, features), BF),
            pltpu.VMEM((hidden, features), BF),
            pltpu.VMEM((LANES * pitch_out, LANES), F32),
            pltpu.SemaphoreType.DMA((groups,)),
            pltpu.SemaphoreType.DMA((groups,)),
            pltpu.SemaphoreType.DMA((3, len(hidden_chunks(hidden)))),
        ],
        compiler_params=pltpu.CompilerParams(vmem_limit_bytes=VMEM_LIMIT),
        cost_estimate=pl.CostEstimate(flops=flops, bytes_accessed=40_000_000, transcendentals=0),
    )(recv, gate_t, up_t, down)


def combine_kernel(
    tiles, pitch, routes_ref, gates_ref, in_hbm, out_ref, score_ref, buffer_ref, stage_ref, sems
):
    features, tokens = out_ref.shape
    peers, rows, _ = in_hbm.shape
    arrivals = group_copies(lambda g: in_hbm.at[g], lambda g: buffer_ref.at[g], sems)
    for copy in arrivals:
        copy.start()
    named, _, rank = route_maps(routes_ref[...])
    gates = gates_ref[...]
    weight = functools.reduce(lambda a, b: a + b, [m * gates[k : k + 1, :] for k, m in enumerate(named)])
    mixed = jnp.concatenate([jnp.where(rank == float(s), weight, 0.0).T for s in range(SLOTS)], axis=1)
    high = mixed.astype(BF)
    low = (mixed - high.astype(F32)).astype(BF)
    both = jnp.concatenate([high, low], axis=0)
    for g, copy in enumerate(arrivals):
        copy.wait()
        for a in range(g * GROUP, (g + 1) * GROUP):
            stage_ref[a * pitch : a * pitch + rows, :] = buffer_ref[a].astype(F32)

    def tile(t):
        return [stage_ref[pl.ds(s * tiles + t, peers, stride=pitch), :] for s in range(SLOTS)]

    for first in range(0, tiles, 2):
        last = min(first + 2, tiles)
        columns = [jnp.concatenate(tile(t), axis=0).astype(BF) for t in range(first, last)]
        part = jnp.dot(both, jnp.concatenate(columns, axis=1), preferred_element_type=F32)
        part = (part[:tokens] + part[tokens:]).T.astype(BF)
        hi = min(last * LANES, features)
        out_ref[first * LANES : hi, :] = part[: hi - first * LANES]
    rest = features - (tiles - 1) * LANES
    scores = [end[:, rest : rest + 1] + end[:, rest + 1 : rest + 2] for end in tile(tiles - 1)]
    for k, m in enumerate(named):
        terms = [jnp.where(rank == float(s), m, 0.0) * scores[s] for s in range(SLOTS)]
        score_ref[k : k + 1, :] = jnp.sum(
            functools.reduce(lambda a, b: a + b, terms), axis=0, keepdims=True
        )


def combine(routes_t, gates_t, recv, features):
    topk, tokens = routes_t.shape
    tiles = -(-features // LANES)
    peers, rows, _ = recv.shape
    pitch = rows + 1
    vmem = pl.BlockSpec(memory_space=pltpu.VMEM)
    return pl.pallas_call(
        functools.partial(combine_kernel, tiles, pitch),
        in_specs=[vmem, vmem, pl.BlockSpec(memory_space=pl.ANY)],
        out_specs=[vmem, vmem],
        out_shape=[
            jax.ShapeDtypeStruct((features, tokens), BF),
            jax.ShapeDtypeStruct((topk, tokens), F32),
        ],
        scratch_shapes=[
            pltpu.VMEM((peers, rows, LANES), BF),
            pltpu.VMEM((peers * pitch, LANES), F32),
            pltpu.SemaphoreType.DMA((peers // GROUP,)),
        ],
        compiler_params=pltpu.CompilerParams(vmem_limit_bytes=VMEM_LIMIT),
    )(routes_t, gates_t, recv)


def exchange(messages):
    return lax.all_to_all(messages, ("node", "local"), split_axis=0, concat_axis=0, tiled=True)


def shards(tokens, out_grad, routes, gates, w_gate, w_up, w_down):
    features = tokens.shape[1]
    routes_t, gates_t = routes.T, gates.T
    gate_t = jnp.swapaxes(w_gate, 1, 2)[0]
    up_t = jnp.swapaxes(w_up, 1, 2)[0]
    recv = exchange(dispatch(routes_t, tokens.T, out_grad.T))
    back = exchange(expert(recv, gate_t, up_t, w_down[0]))
    input_grad_t, gate_grad_t = combine(routes_t, gates_t, back, features)
    return (input_grad_t.T, gate_grad_t.T)


def solution(mesh):
    both = ("node", "local")
    return jax.shard_map(
        shards,
        mesh=mesh,
        in_specs=(P(both, None),) * 4 + (P(both, None, None),) * 3,
        out_specs=(P(both, None), P(both, None)),
        check_vma=False,
    )
```

time: 226 us -> 212 us (0.938)
  Pallas kernels: 67.5 us -> 53.1 us
    pallas_call x1, Pallas kernels: 51.1 us -> 42.1 us  [expert(): pl.pallas_call(functools.partial(expert_kernel, tiles, pitch_in, pitch_ou...]
    pallas_call x2, Pallas kernels: 16.4 us -> 11 us  [the longest x1 5.76 us: dispatch(): pl.pallas_call(functools.partial(dispatch_kernel, tiles, pitch), in_specs...]
where the time goes in v2:
time: 212 us; the launch traced here: 211 us
  blocking collectives  157 us (74%)
  Pallas kernels  53.1 us (25%)
    all_to_all x2, blocking collectives, exchange(): lax.all_to_all(messages, ('node', 'local'), split_axis=0, concat_axis=0,...  157 us
    pallas_call x1, Pallas kernels, expert(): pl.pallas_call(functools.partial(expert_kernel, tiles, pitch_in, pitch_ou...  42.1 us
    pallas_call x1, Pallas kernels, dispatch(): pl.pallas_call(functools.partial(dispatch_kernel, tiles, pitch), in_specs...  5.76 us
    pallas_call x1, Pallas kernels, combine(): pl.pallas_call(functools.partial(combine_kernel, tiles, pitch), in_specs=...  5.26 us

profile of v2, /device:TPU:1, one launch (start us, length us, event | category | flops | bytes accessed | tf_op | source)
XLA Modules:
  0.0 211.3 jit_solution(9874082260746663730)
XLA Ops:
  0.6 5.8 %shard_map.86 = bf16[128,232,128]{2,1,0:T(8,128)(2,1)} custom-call(s32[4,128]{1,0:T(4,128)} %bitcast.15, bf16[2880,128]{1,0:T(8,128)(2,1)} %bitcast.13, bf16[2880,128]{1,0:T(8,128)(2,1)} %bitcast.14), custom_call_target="tpu_custom_call" | custom-call | tf_op jit(solution)/shard_map/pallas_call | solution.py:91
  6.4 101.2 %all_to_all.10.in_hbm = bf16[128,232,128]{2,1,0:T(8,128)(2,1)} all-to-all(bf16[128,232,128]{2,1,0:T(8,128)(2,1)} %shard_map.86), channel_id=1, replica_groups=mesh['node'=16,'local'=8] {'node','local'}, dimensions={0} | all-to-all | bytes 15204352 | tf_op jit(solution)/shard_map/all_to_all | solution.py:300
  107.5 42.1 %shard_map.87 = bf16[128,120,128]{2,1,0:T(8,128)(2,1)} custom-call(bf16[128,232,128]{2,1,0:T(8,128)(2,1)} %all_to_all.10.in_hbm, bf16[1440,2880]{1,0:T(8,128)(2,1)} %bitcast.18, bf16[1440,2880]{1,0:T(8,128)(2,1)} %bitcast.19, bf16[1440,2880]{1,0:T(8,128)(2,1)} %bitcast.20), custom_call_target="tpu_custom_call" | custom-call | flops 26542080000 | bytes 40000000 | tf_op jit(solution)/shard_map/pallas_call | solution.py:214
  149.7 56.2 %all_to_all.11.in_hbm = bf16[128,120,128]{2,1,0:T(8,128)(2,1)} all-to-all(bf16[128,120,128]{2,1,0:T(8,128)(2,1)} %shard_map.87), channel_id=1, replica_groups=mesh['node'=16,'local'=8] {'node','local'}, dimensions={0} | all-to-all | bytes 7864320 | tf_op jit(solution)/shard_map/all_to_all | solution.py:300
  205.8 5.3 %shard_map.88 = (bf16[2880,128]{1,0:T(8,128)(2,1)}, f32[4,128]{1,0:T(4,128)}) custom-call(s32[4,128]{1,0:T(4,128)} %bitcast.16, f32[4,128]{1,0:T(4,128)} %bitcast.17, bf16[128,120,128]{2,1,0:T(8,128)(2,1)} %all_to_all.11.in_hbm), custom_call_target="tpu_custom_call" | custom-call | tf_op jit(solution)/shard_map/pallas_call | solution.py:282

commit v3 on v2

v3 whole, which is shorter than its diff:
```python
import functools

import jax
import jax.numpy as jnp
from jax import lax
from jax.experimental import pallas as pl
from jax.experimental.pallas import tpu as pltpu
from jax.sharding import PartitionSpec as P

LANES = 128
GROUP = 16
SLOTS = 5
PARTS = 4
BF = jnp.bfloat16
F32 = jnp.float32
NT = (((1,), (1,)), ((), ()))
SMALL_LIMIT = 14 * 1024 * 1024
EXPERT_LIMIT = 33 * 1024 * 1024


def round_up(value, step):
    return -(-value // step) * step


def route_maps(routes_t):
    topk, tokens = routes_t.shape
    expert = lax.broadcasted_iota(jnp.int32, (LANES, tokens), 0)
    named = [jnp.where(routes_t[k : k + 1, :] == expert, 1.0, 0.0) for k in range(topk)]
    total = functools.reduce(lambda a, b: a + b, named)
    row = lax.broadcasted_iota(jnp.int32, (tokens, tokens), 0)
    column = lax.broadcasted_iota(jnp.int32, (tokens, tokens), 1)
    earlier = jnp.where(row < column, 1.0, 0.0).astype(BF)
    rank = jnp.dot(total.astype(BF), earlier, preferred_element_type=F32)
    return named, total, rank


def pack_messages(stage_ref, base, out_ref, rows, pitch, begin, end):
    for a in range(begin, end):
        first = base + (a - begin) * pitch
        out_ref[a] = stage_ref[first : first + rows, :].astype(BF)


def in_vmem(value):
    return pltpu.with_memory_space_constraint(value, pltpu.VMEM)


def dispatch_kernel(
    tiles, pitch, routes_hbm, tok_hbm, grad_hbm, out_ref, routes_ref, tok_ref, grad_ref, stage_ref, sems
):
    copies = [
        pltpu.make_async_copy(src, dst, sems.at[i])
        for i, (src, dst) in enumerate(
            ((routes_hbm, routes_ref), (tok_hbm, tok_ref), (grad_hbm, grad_ref))
        )
    ]
    for copy in copies:
        copy.start()
    copies[0].wait()
    features = tok_ref.shape[0]
    peers, rows, _ = out_ref.shape
    _, total, rank = route_maps(routes_ref[...])
    place = [jnp.where(rank == float(s), total, 0.0).astype(BF) for s in range(SLOTS)]

    def part_of(begin, base):
        rows_of = jnp.concatenate([p[begin : begin + count] for p in place], axis=0)
        for j, ref in enumerate((tok_ref, grad_ref)):
            for lo in range(0, features, 256):
                hi = min(lo + 256, features)
                part = lax.dot_general(rows_of, ref[lo:hi, :], NT, preferred_element_type=F32)
                if (hi - lo) % LANES:
                    part = jnp.concatenate(
                        [part, jnp.zeros((part.shape[0], LANES - (hi - lo) % LANES), F32)], axis=1
                    )
                for s in range(SLOTS):
                    for t in range(part.shape[1] // LANES):
                        row = base + (j * SLOTS + s) * tiles + lo // LANES + t
                        stage_ref[pl.ds(row, count, stride=pitch), :] = part[
                            s * count : (s + 1) * count, t * LANES : (t + 1) * LANES
                        ]

    count = peers // PARTS
    for row in range(2 * SLOTS * tiles, rows):
        stage_ref[pl.ds(row, 2 * count, stride=pitch), :] = jnp.zeros((2 * count, LANES), F32)
    copies[1].wait()
    copies[2].wait()
    for part in range(PARTS):
        base = part % 2 * count * pitch
        part_of(part * count, base)
        pack_messages(stage_ref, base, out_ref, rows, pitch, part * count, (part + 1) * count)


def dispatch(routes_t, tok_t, grad_t):
    features, tokens = tok_t.shape
    tiles = -(-features // LANES)
    rows = round_up(2 * SLOTS * tiles, 8)
    pitch = rows + 1
    return pl.pallas_call(
        functools.partial(dispatch_kernel, tiles, pitch),
        in_specs=[pl.BlockSpec(memory_space=pltpu.HBM)] * 3,
        out_specs=pl.BlockSpec(memory_space=pltpu.VMEM),
        out_shape=pltpu.VMEM((LANES, rows, LANES), BF),
        scratch_shapes=[
            pltpu.VMEM(routes_t.shape, routes_t.dtype),
            pltpu.VMEM(tok_t.shape, BF),
            pltpu.VMEM(grad_t.shape, BF),
            pltpu.VMEM((2 * LANES // PARTS * pitch, LANES), F32),
            pltpu.SemaphoreType.DMA((3,)),
        ],
        compiler_params=pltpu.CompilerParams(vmem_limit_bytes=SMALL_LIMIT),
    )(*[pltpu.with_memory_space_constraint(v, pltpu.HBM) for v in (routes_t, tok_t, grad_t)])


def expert_kernel(
    tiles, pitch_in, pitch_out, in_ref, gate_ref, up_ref, down_hbm, out_ref,
    rows_ref, pre_ref, upg_ref, down_ref, stage_ref, sem,
):
    peers, rows_in, _ = in_ref.shape
    rows_out = out_ref.shape[1]
    hidden, features = gate_ref.shape
    wide = SLOTS * peers
    chunks = [(lo, min(lo + 512, hidden)) for lo in range(0, hidden, 512)]
    arrival = pltpu.make_async_copy(down_hbm, down_ref, sem)
    arrival.start()
    first_row = [0, (SLOTS * tiles) // 16 * 16]

    def unpack(j, g):
        start, count = first_row[j], rows_in - first_row[1]
        base = g * GROUP * pitch_out
        for a in range(GROUP):
            stage_ref[base + a * pitch_out : base + a * pitch_out + count, :] = in_ref[
                g * GROUP + a, start : start + count
            ].astype(F32)
        for s in range(SLOTS):
            for t in range(tiles):
                row = base + (j * SLOTS + s) * tiles + t - start
                value = stage_ref[pl.ds(row, GROUP, stride=pitch_out), :]
                first = s * peers + g * GROUP
                rows_ref[j, first : first + GROUP, t * LANES : (t + 1) * LANES] = value.astype(BF)

    for g in range(peers // GROUP):
        unpack(0, g)

    score = jnp.zeros((wide, 1), F32)
    for c, (lo, hi) in enumerate(chunks):
        x = rows_ref[0, :, :features]
        gate_pre = lax.dot_general(x, gate_ref[lo:hi, :], NT, preferred_element_type=F32)
        up_pre = lax.dot_general(x, up_ref[lo:hi, :], NT, preferred_element_type=F32)
        if c == 0:
            for g in range(peers // GROUP):
                unpack(1, g)
            arrival.wait()
        hidden_grad = lax.dot_general(
            rows_ref[1, :, :features], down_ref[lo:hi, :], NT, preferred_element_type=F32
        )
        sig = jax.nn.sigmoid(gate_pre)
        act = gate_pre * sig
        act_up = (act * up_pre).astype(BF).astype(F32)
        score = score + jnp.sum(act_up * hidden_grad, axis=1, keepdims=True)
        upg_ref[:, lo:hi] = (hidden_grad * act).astype(BF)
        pre_ref[:, lo:hi] = (hidden_grad * up_pre * sig * (1.0 + gate_pre * (1.0 - sig))).astype(BF)
    high = score.astype(BF).astype(F32)
    low = score - high

    def place(value, row):
        for s in range(SLOTS):
            stage_ref[pl.ds(s * tiles + row, peers, stride=pitch_out), :] = value[
                s * peers : (s + 1) * peers
            ]

    def columns(lo, width):
        back = jnp.dot(pre_ref[...], gate_ref[:, pl.ds(lo, width)], preferred_element_type=F32)
        return back + jnp.dot(upg_ref[...], up_ref[:, pl.ds(lo, width)], preferred_element_type=F32)

    for row in range(SLOTS * tiles, rows_out):
        stage_ref[pl.ds(row, peers, stride=pitch_out), :] = jnp.zeros((peers, LANES), F32)
    whole = features // 256

    for n in range(whole):
        part = columns(n * 256, 256)
        place(part[:, :LANES], 2 * n)
        place(part[:, LANES:], 2 * n + 1)

    rest = features - whole * 256
    lane = lax.broadcasted_iota(jnp.int32, (wide, LANES - rest), 1)
    scores = jnp.where(lane == 0, high, jnp.where(lane == 1, low, 0.0))
    place(jnp.concatenate([columns(whole * 256, rest), scores], axis=1), 2 * whole)
    pack_messages(stage_ref, 0, out_ref, rows_out, pitch_out, 0, peers)


def expert(recv, gate_t, up_t, down):
    peers, rows_in, _ = recv.shape
    hidden, features = gate_t.shape
    tiles = -(-features // LANES)
    rows_out = round_up(SLOTS * tiles, 8)
    pitch_in, pitch_out = rows_in + 1, rows_out + 1
    wide = SLOTS * LANES
    flops = 5 * 2 * wide * hidden * features
    return pl.pallas_call(
        functools.partial(expert_kernel, tiles, pitch_in, pitch_out),
        in_specs=[pl.BlockSpec(memory_space=pltpu.VMEM)] * 3 + [pl.BlockSpec(memory_space=pl.ANY)],
        out_specs=pl.BlockSpec(memory_space=pltpu.VMEM),
        out_shape=pltpu.VMEM((peers, rows_out, LANES), BF),
        scratch_shapes=[
            pltpu.VMEM((2, wide, tiles * LANES), BF),
            pltpu.VMEM((wide, hidden), BF),
            pltpu.VMEM((wide, hidden), BF),
            pltpu.VMEM((hidden, features), BF),
            pltpu.VMEM((LANES * pitch_out, LANES), F32),
            pltpu.SemaphoreType.DMA,
        ],
        compiler_params=pltpu.CompilerParams(vmem_limit_bytes=EXPERT_LIMIT),
        cost_estimate=pl.CostEstimate(flops=flops, bytes_accessed=40_000_000, transcendentals=0),
    )(in_vmem(recv), in_vmem(gate_t), in_vmem(up_t), down)


def combine_kernel(
    tiles, pitch, routes_ref, gates_ref, in_ref, out_ref, score_ref, stage_ref
):
    features, tokens = out_ref.shape
    peers, rows, _ = in_ref.shape
    named, _, rank = route_maps(routes_ref[...])
    gates = gates_ref[...]
    weight = functools.reduce(lambda a, b: a + b, [m * gates[k : k + 1, :] for k, m in enumerate(named)])
    mixed = jnp.concatenate([jnp.where(rank == float(s), weight, 0.0).T for s in range(SLOTS)], axis=1)
    high = mixed.astype(BF)
    low = (mixed - high.astype(F32)).astype(BF)
    both = jnp.concatenate([high, low], axis=0)
    for a in range(peers):
        stage_ref[a * pitch : a * pitch + rows, :] = in_ref[a].astype(F32)

    def tile(t):
        return [stage_ref[pl.ds(s * tiles + t, peers, stride=pitch), :] for s in range(SLOTS)]

    for first in range(0, tiles, 2):
        last = min(first + 2, tiles)
        columns = [jnp.concatenate(tile(t), axis=0).astype(BF) for t in range(first, last)]
        part = jnp.dot(both, jnp.concatenate(columns, axis=1), preferred_element_type=F32)
        part = (part[:tokens] + part[tokens:]).T.astype(BF)
        hi = min(last * LANES, features)
        out_ref[first * LANES : hi, :] = part[: hi - first * LANES]
    rest = features - (tiles - 1) * LANES
    scores = [end[:, rest : rest + 1] + end[:, rest + 1 : rest + 2] for end in tile(tiles - 1)]
    for k, m in enumerate(named):
        terms = [jnp.where(rank == float(s), m, 0.0) * scores[s] for s in range(SLOTS)]
        score_ref[k : k + 1, :] = jnp.sum(
            functools.reduce(lambda a, b: a + b, terms), axis=0, keepdims=True
        )


def combine(routes_t, gates_t, recv, features):
    topk, tokens = routes_t.shape
    tiles = -(-features // LANES)
    peers, rows, _ = recv.shape
    pitch = rows + 1
    vmem = pl.BlockSpec(memory_space=pltpu.VMEM)
    return pl.pallas_call(
        functools.partial(combine_kernel, tiles, pitch),
        in_specs=[vmem, vmem, vmem],
        out_specs=[vmem, vmem],
        out_shape=[
            jax.ShapeDtypeStruct((features, tokens), BF),
            jax.ShapeDtypeStruct((topk, tokens), F32),
        ],
        scratch_shapes=[
            pltpu.VMEM((peers * pitch, LANES), F32),
        ],
        compiler_params=pltpu.CompilerParams(vmem_limit_bytes=SMALL_LIMIT),
    )(routes_t, gates_t, in_vmem(recv))


def exchange(messages):
    return lax.all_to_all(messages, ("node", "local"), split_axis=0, concat_axis=0, tiled=True)


def shards(tokens, out_grad, routes, gates, w_gate, w_up, w_down):
    features = tokens.shape[1]
    routes_t, gates_t = routes.T, gates.T
    gate_t = jnp.swapaxes(w_gate, 1, 2)[0]
    up_t = jnp.swapaxes(w_up, 1, 2)[0]
    send = dispatch(routes_t, tokens.T, out_grad.T)
    send, gate_t, up_t = lax.optimization_barrier((send, gate_t, up_t))
    recv = exchange(send)
    back = exchange(expert(recv, gate_t, up_t, w_down[0]))
    input_grad_t, gate_grad_t = combine(routes_t, gates_t, back, features)
    return (input_grad_t.T, gate_grad_t.T)


def solution(mesh):
    both = ("node", "local")
    return jax.shard_map(
        shards,
        mesh=mesh,
        in_specs=(P(both, None),) * 4 + (P(both, None, None),) * 3,
        out_specs=(P(both, None), P(both, None)),
        check_vma=False,
    )
```

time: 212 us -> 199 us (0.939)
  Pallas kernels: 53.1 us -> 41.7 us
    pallas_call x1, Pallas kernels: 42.1 us -> 34.6 us  [expert(): pl.pallas_call(functools.partial(expert_kernel, tiles, pitch_in, pitch_ou...]
    pallas_call x1, Pallas kernels: 5.26 us -> 2.94 us  [combine(): pl.pallas_call(functools.partial(combine_kernel, tiles, pitch), in_specs=...]
where the time goes in v3:
time: 199 us
  blocking collectives  157 us (79%)
  Pallas kernels  41.7 us (21%)
    all_to_all x2, blocking collectives, exchange(): lax.all_to_all(messages, ('node', 'local'), split_axis=0, concat_axis=0,...  157 us
    pallas_call x1, Pallas kernels, expert(): pl.pallas_call(functools.partial(expert_kernel, tiles, pitch_in, pitch_ou...  34.6 us
    pallas_call x1, Pallas kernels, dispatch(): pl.pallas_call(functools.partial(dispatch_kernel, tiles, pitch), in_specs...  4.21 us

profile of v3, /device:TPU:1, one launch (start us, length us, event | category | flops | bytes accessed | tf_op | source)
XLA Modules:
  0.0 199.3 jit_solution(12119217316813329643)
XLA Ops:
  0.6 0.0 slice-start
  0.6 0.0 slice-start.1
  0.7 0.0 slice-start.3
  0.7 0.0 slice-start.4
  0.7 4.2 %shard_map.86 = bf16[128,232,128]{2,1,0:T(8,128)(2,1)S(1)} custom-call(s32[4,128]{1,0:T(4,128)} %bitcast.13, bf16[2880,128]{1,0:T(8,128)(2,1)} %bitcast.22, bf16[2880,128]{1,0:T(8,128)(2,1)} %bitcast.23), custom_call_target="tpu_custom_call" | custom-call | tf_op jit(solution)/shard_map/pallas_call | solution.py:97
  4.9 0.0 slice-start.2
  4.9 0.0 slice-start.5
  4.9 100.8 %all_to_all.10.in_ref = bf16[128,232,128]{2,1,0:T(8,128)(2,1)S(1)} all-to-all(bf16[128,232,128]{2,1,0:T(8,128)(2,1)S(1)} %shard_map.86), channel_id=1, replica_groups=mesh['node'=16,'local'=8] {'node','local'}, dimensions={0} | all-to-all | bytes 15204352 | tf_op jit(solution)/shard_map/all_to_all | solution.py:272
  105.8 0.0 slice-done
  105.8 0.0 slice-done.1
  105.8 0.0 slice-done.3
  105.8 0.0 slice-done.4
  105.8 0.0 slice-done.2
  105.8 0.0 slice-done.5
  105.8 34.6 %shard_map.87 = bf16[128,120,128]{2,1,0:T(8,128)(2,1)S(1)} custom-call(bf16[128,232,128]{2,1,0:T(8,128)(2,1)S(1)} %all_to_all.10.in_ref, bf16[1440,2880]{1,0:T(8,128)(2,1)S(1)} %bitcast.18, bf16[1440,2880]{1,0:T(8,128)(2,1)S(1)} %bitcast.21, bf16[1440,2880]{1,0:T(8,128)(2,1)} %bitcast.24), custom_call_target="tpu_custom_call" | custom-call | flops 26542080000 | bytes 40000000 | tf_op jit(solution)/shard_map/pallas_call | solution.py:198
  140.4 0.0 copy-start
  140.4 0.0 copy-start.1
  140.5 55.9 %all_to_all.11.in_ref = bf16[128,120,128]{2,1,0:T(8,128)(2,1)S(1)} all-to-all(bf16[128,120,128]{2,1,0:T(8,128)(2,1)S(1)} %shard_map.87), channel_id=1, replica_groups=mesh['node'=16,'local'=8] {'node','local'}, dimensions={0} | all-to-all | bytes 7864320 | tf_op jit(solution)/shard_map/all_to_all | solution.py:272
  196.3 0.0 copy-done
  196.3 0.0 copy-done.1
  196.3 2.9 %shard_map.88 = (bf16[2880,128]{1,0:T(8,128)(2,1)}, f32[4,128]{1,0:T(4,128)}) custom-call(s32[4,128]{1,0:T(4,128)S(1)} %bitcast.14, f32[4,128]{1,0:T(4,128)S(1)} %bitcast.15, bf16[128,120,128]{2,1,0:T(8,128)(2,1)S(1)} %all_to_all.11.in_ref), custom_call_target="tpu_custom_call" | custom-call | tf_op jit(solution)/shard_map/pallas_call | solution.py:256
  (2 shorter events, 0.0 us)
Async XLA Ops:
  0.6 105.1 %slice-start = ((s8[8478720]{0:T(1024)(128)(4,1)}), s8[4194304]{0:T(1024)(128)(4,1)S(1)}, s32[]{:S(2)}) async-start(s8[8478720]{0:T(1024)(128)(4,1)} %bitcast.16), calls=%async_computation.2 | async-start | bytes 8388608
  0.6 105.1 %slice-start.1 = ((s8[8478720]{0:T(1024)(128)(4,1)}), s8[4194304]{0:T(1024)(128)(4,1)S(1)}, s32[]{:S(2)}) async-start(s8[8478720]{0:T(1024)(128)(4,1)} %bitcast.16), calls=%async_computation.3 | async-start | bytes 8388608
  0.7 105.1 %slice-start.3 = ((s8[8478720]{0:T(1024)(128)(4,1)}), s8[4194304]{0:T(1024)(128)(4,1)S(1)}, s32[]{:S(2)}) async-start(s8[8478720]{0:T(1024)(128)(4,1)} %bitcast.19), calls=%async_computation.5 | async-start | bytes 8388608
  0.7 105.1 %slice-start.4 = ((s8[8478720]{0:T(1024)(128)(4,1)}), s8[4194304]{0:T(1024)(128)(4,1)S(1)}, s32[]{:S(2)}) async-start(s8[8478720]{0:T(1024)(128)(4,1)} %bitcast.19), calls=%async_computation.6 | async-start | bytes 8388608
  4.9 100.9 %slice-start.2 = ((s8[8478720]{0:T(1024)(128)(4,1)}), s8[90112]{0:T(1024)(128)(4,1)S(1)}, s32[]{:S(2)}) async-start(s8[8478720]{0:T(1024)(128)(4,1)} %bitcast.16), calls=%async_computation.4 | async-start | bytes 180224
  4.9 100.9 %slice-start.5 = ((s8[8478720]{0:T(1024)(128)(4,1)}), s8[90112]{0:T(1024)(128)(4,1)S(1)}, s32[]{:S(2)}) async-start(s8[8478720]{0:T(1024)(128)(4,1)} %bitcast.19), calls=%async_computation.7 | async-start | bytes 180224
  140.4 55.9 %copy-start = (s32[128,4]{0,1:T(4,128)S(1)}, s32[128,4]{0,1:T(4,128)}, u32[]{:S(2)}) copy-start(s32[128,4]{0,1:T(4,128)} %param.9) | copy-start | bytes 6148
  140.4 55.9 %copy-start.1 = (f32[128,4]{0,1:T(4,128)S(1)}, f32[128,4]{0,1:T(4,128)}, u32[]{:S(2)}) copy-start(f32[128,4]{0,1:T(4,128)} %param.10) | copy-start | bytes 6148

commit v4 on v3

--- a/solution.py
+++ b/solution.py
@@ -10,6 +10,9 @@
 LANES = 128
 GROUP = 16
 SLOTS = 5
+FOLD = 2
+BLOCK = 128
+HALF = LANES // 2
 PARTS = 4
 BF = jnp.bfloat16
 F32 = jnp.float32
@@ -38,6 +41,11 @@
     for a in range(begin, end):
         first = base + (a - begin) * pitch
         out_ref[a] = stage_ref[first : first + rows, :].astype(BF)
+
+
+def copy_rows(source_ref, target_ref, kind):
+    for row in range(0, source_ref.shape[0], BLOCK):
+        target_ref[row : row + BLOCK, :] = source_ref[row : row + BLOCK, :].astype(kind)
 
 
 def in_vmem(value):
@@ -115,25 +123,27 @@
     rows_ref, pre_ref, upg_ref, down_ref, stage_ref, sem,
 ):
     peers, rows_in, _ = in_ref.shape
-    rows_out = out_ref.shape[1]
+    rows_out = out_ref.shape[0] // peers
     hidden, features = gate_ref.shape
     wide = SLOTS * peers
     chunks = [(lo, min(lo + 512, hidden)) for lo in range(0, hidden, 512)]
     arrival = pltpu.make_async_copy(down_hbm, down_ref, sem)
     arrival.start()
+    whole = features // LANES
     first_row = [0, (SLOTS * tiles) // 16 * 16]
 
     def unpack(j, g):
         start, count = first_row[j], rows_in - first_row[1]
-        base = g * GROUP * pitch_out
+        pitch = count + 1
+        base = g * GROUP * pitch
         for a in range(GROUP):
-            stage_ref[base + a * pitch_out : base + a * pitch_out + count, :] = in_ref[
+            stage_ref[base + a * pitch : base + a * pitch + count, :] = in_ref[
                 g * GROUP + a, start : start + count
             ].astype(F32)
         for s in range(SLOTS):
             for t in range(tiles):
                 row = base + (j * SLOTS + s) * tiles + t - start
-                value = stage_ref[pl.ds(row, GROUP, stride=pitch_out), :]
+                value = stage_ref[pl.ds(row, GROUP, stride=pitch), :]
                 first = s * peers + g * GROUP
                 rows_ref[j, first : first + GROUP, t * LANES : (t + 1) * LANES] = value.astype(BF)
 
@@ -161,51 +171,53 @@
     high = score.astype(BF).astype(F32)
     low = score - high
 
-    def place(value, row):
-        for s in range(SLOTS):
-            stage_ref[pl.ds(s * tiles + row, peers, stride=pitch_out), :] = value[
-                s * peers : (s + 1) * peers
-            ]
+    def place(value, s, t):
+        stage_ref[pl.ds(s * whole + t, peers, stride=pitch_out), :] = value
 
     def columns(lo, width):
         back = jnp.dot(pre_ref[...], gate_ref[:, pl.ds(lo, width)], preferred_element_type=F32)
         return back + jnp.dot(upg_ref[...], up_ref[:, pl.ds(lo, width)], preferred_element_type=F32)
 
-    for row in range(SLOTS * tiles, rows_out):
-        stage_ref[pl.ds(row, peers, stride=pitch_out), :] = jnp.zeros((peers, LANES), F32)
-    whole = features // 256
-
-    for n in range(whole):
-        part = columns(n * 256, 256)
-        place(part[:, :LANES], 2 * n)
-        place(part[:, LANES:], 2 * n + 1)
-
-    rest = features - whole * 256
-    lane = lax.broadcasted_iota(jnp.int32, (wide, LANES - rest), 1)
-    scores = jnp.where(lane == 0, high, jnp.where(lane == 1, low, 0.0))
-    place(jnp.concatenate([columns(whole * 256, rest), scores], axis=1), 2 * whole)
-    pack_messages(stage_ref, 0, out_ref, rows_out, pitch_out, 0, peers)
+    for lo in range(0, whole * LANES, 256):
+        part = columns(lo, 256)
+        for s in range(SLOTS):
+            for t in range(2):
+                place(part[s * peers : (s + 1) * peers, t * LANES : (t + 1) * LANES], s, lo // LANES + t)
+    part = columns(whole * LANES, HALF)
+    lane = lax.broadcasted_iota(jnp.int32, (peers, HALF), 1)
+    halves = [part[s * peers : (s + 1) * peers] for s in range(SLOTS)]
+    scores = jnp.zeros((peers, HALF), F32)
+    for s in range(SLOTS):
+        rows = slice(s * peers, (s + 1) * peers)
+        scores = jnp.where(lane == 2 * s, high[rows], jnp.where(lane == 2 * s + 1, low[rows], scores))
+    halves.append(scores)
+    for pair in range(len(halves) // 2):
+        place(jnp.concatenate(halves[2 * pair : 2 * pair + 2], axis=1), SLOTS, pair)
+    for row in range(SLOTS * whole + len(halves) // 2, rows_out):
+        place(jnp.zeros((peers, LANES), F32), 0, row)
+    for row in range(0, out_ref.shape[0], BLOCK):
+        out_ref[row : row + BLOCK, :] = stage_ref[row : row + BLOCK, :].astype(BF)
 
 
 def expert(recv, gate_t, up_t, down):
     peers, rows_in, _ = recv.shape
     hidden, features = gate_t.shape
     tiles = -(-features // LANES)
-    rows_out = round_up(SLOTS * tiles, 8)
-    pitch_in, pitch_out = rows_in + 1, rows_out + 1
+    rows_out = round_up(SLOTS * (tiles - 1) + (SLOTS + 1) // 2, FOLD)
+    pitch_in, pitch_out = rows_in + 1, rows_out
     wide = SLOTS * LANES
     flops = 5 * 2 * wide * hidden * features
     return pl.pallas_call(
         functools.partial(expert_kernel, tiles, pitch_in, pitch_out),
         in_specs=[pl.BlockSpec(memory_space=pltpu.VMEM)] * 3 + [pl.BlockSpec(memory_space=pl.ANY)],
         out_specs=pl.BlockSpec(memory_space=pltpu.VMEM),
-        out_shape=pltpu.VMEM((peers, rows_out, LANES), BF),
+        out_shape=pltpu.VMEM((peers * rows_out, LANES), BF),
         scratch_shapes=[
             pltpu.VMEM((2, wide, tiles * LANES), BF),
             pltpu.VMEM((wide, hidden), BF),
             pltpu.VMEM((wide, hidden), BF),
             pltpu.VMEM((hidden, features), BF),
-            pltpu.VMEM((LANES * pitch_out, LANES), F32),
+            pltpu.VMEM((LANES * (rows_out + 7), LANES), F32),
             pltpu.SemaphoreType.DMA,
         ],
         compiler_params=pltpu.CompilerParams(vmem_limit_bytes=EXPERT_LIMIT),
@@ -217,7 +229,7 @@
     tiles, pitch, routes_ref, gates_ref, in_ref, out_ref, score_ref, stage_ref
 ):
     features, tokens = out_ref.shape
-    peers, rows, _ = in_ref.shape
+    peers = LANES
     named, _, rank = route_maps(routes_ref[...])
     gates = gates_ref[...]
     weight = functools.reduce(lambda a, b: a + b, [m * gates[k : k + 1, :] for k, m in enumerate(named)])
@@ -225,11 +237,17 @@
     high = mixed.astype(BF)
     low = (mixed - high.astype(F32)).astype(BF)
     both = jnp.concatenate([high, low], axis=0)
-    for a in range(peers):
-        stage_ref[a * pitch : a * pitch + rows, :] = in_ref[a].astype(F32)
+    copy_rows(in_ref, stage_ref, F32)
+    whole = tiles - 1
+    pairs = [
+        stage_ref[pl.ds(SLOTS * whole + pair, peers, stride=pitch), :] for pair in range((SLOTS + 1) // 2)
+    ]
+    ends = [pairs[s // 2] if s % 2 == 0 else pltpu.roll(pairs[s // 2], HALF, 1) for s in range(SLOTS + 1)]
 
     def tile(t):
-        return [stage_ref[pl.ds(s * tiles + t, peers, stride=pitch), :] for s in range(SLOTS)]
+        if t == whole:
+            return ends[:SLOTS]
+        return [stage_ref[pl.ds(s * whole + t, peers, stride=pitch), :] for s in range(SLOTS)]
 
     for first in range(0, tiles, 2):
         last = min(first + 2, tiles)
@@ -238,8 +256,7 @@
         part = (part[:tokens] + part[tokens:]).T.astype(BF)
         hi = min(last * LANES, features)
         out_ref[first * LANES : hi, :] = part[: hi - first * LANES]
-    rest = features - (tiles - 1) * LANES
-    scores = [end[:, rest : rest + 1] + end[:, rest + 1 : rest + 2] for end in tile(tiles - 1)]
+    scores = [ends[-1][:, 2 * s : 2 * s + 1] + ends[-1][:, 2 * s + 1 : 2 * s + 2] for s in range(SLOTS)]
     for k, m in enumerate(named):
         terms = [jnp.where(rank == float(s), m, 0.0) * scores[s] for s in range(SLOTS)]
         score_ref[k : k + 1, :] = jnp.sum(
@@ -250,8 +267,7 @@
 def combine(routes_t, gates_t, recv, features):
     topk, tokens = routes_t.shape
     tiles = -(-features // LANES)
-    peers, rows, _ = recv.shape
-    pitch = rows + 1
+    pitch = recv.shape[0] // LANES
     vmem = pl.BlockSpec(memory_space=pltpu.VMEM)
     return pl.pallas_call(
         functools.partial(combine_kernel, tiles, pitch),
@@ -262,7 +278,7 @@
             jax.ShapeDtypeStruct((topk, tokens), F32),
         ],
         scratch_shapes=[
-            pltpu.VMEM((peers * pitch, LANES), F32),
+            pltpu.VMEM(recv.shape, F32),
         ],
         compiler_params=pltpu.CompilerParams(vmem_limit_bytes=SMALL_LIMIT),
     )(routes_t, gates_t, in_vmem(recv))
@@ -280,7 +296,10 @@
     send = dispatch(routes_t, tokens.T, out_grad.T)
     send, gate_t, up_t = lax.optimization_barrier((send, gate_t, up_t))
     recv = exchange(send)
-    back = exchange(expert(recv, gate_t, up_t, w_down[0]))
+    back = expert(recv, gate_t, up_t, w_down[0])
+    peers = recv.shape[0]
+    rows = back.shape[0] // peers
+    back = exchange(back.reshape(peers, rows // FOLD, FOLD, LANES)).reshape(back.shape)
     input_grad_t, gate_grad_t = combine(routes_t, gates_t, back, features)
     return (input_grad_t.T, gate_grad_t.T)
 

time: 199 us -> 197 us (0.990)
  blocking collectives: 157 us -> 155 us
    all_to_all x2, blocking collectives: 157 us -> 155 us  [exchange(): lax.all_to_all(messages, ('node', 'local'), split_axis=0, concat_axis=0,...]
where the time goes in v4:
time: 197 us
  blocking collectives  155 us (79%)
  Pallas kernels  41.7 us (21%)
    all_to_all x2, blocking collectives, exchange(): lax.all_to_all(messages, ('node', 'local'), split_axis=0, concat_axis=0,...  155 us
    pallas_call x1, Pallas kernels, expert(): pl.pallas_call(functools.partial(expert_kernel, tiles, pitch_in, pitch_ou...  34.7 us
    pallas_call x1, Pallas kernels, dispatch(): pl.pallas_call(functools.partial(dispatch_kernel, tiles, pitch), in_specs...  4.21 us

profile of v4, /device:TPU:1, one launch (start us, length us, event | category | flops | bytes accessed | tf_op | source)
XLA Modules:
  0.0 197.1 jit_solution(17035355022276431332)
XLA Ops:
  0.6 0.0 slice-start
  0.6 0.0 slice-start.1
  0.7 0.0 slice-start.3
  0.7 0.0 slice-start.4
  0.7 4.2 %shard_map.86 = bf16[128,232,128]{2,1,0:T(8,128)(2,1)S(1)} custom-call(s32[4,128]{1,0:T(4,128)} %bitcast.17, bf16[2880,128]{1,0:T(8,128)(2,1)} %bitcast.26, bf16[2880,128]{1,0:T(8,128)(2,1)} %bitcast.27), custom_call_target="tpu_custom_call" | custom-call | tf_op jit(solution)/shard_map/pallas_call | solution.py:105
  4.9 0.0 slice-start.2
  4.9 0.0 slice-start.5
  4.9 100.8 %all_to_all.10.in_ref = bf16[128,232,128]{2,1,0:T(8,128)(2,1)S(1)} all-to-all(bf16[128,232,128]{2,1,0:T(8,128)(2,1)S(1)} %shard_map.86), channel_id=1, replica_groups=mesh['node'=16,'local'=8] {'node','local'}, dimensions={0} | all-to-all | bytes 15204352 | tf_op jit(solution)/shard_map/all_to_all | solution.py:288
  105.8 0.0 slice-done
  105.8 0.0 slice-done.1
  105.8 0.0 slice-done.3
  105.8 0.0 slice-done.4
  105.8 0.0 slice-done.2
  105.8 0.0 slice-done.5
  105.8 0.0 copy-start
  105.8 0.0 copy-start.1
  105.9 34.7 %shard_map.87 = bf16[14592,128]{1,0:T(8,128)(2,1)S(1)} custom-call(bf16[128,232,128]{2,1,0:T(8,128)(2,1)S(1)} %all_to_all.10.in_ref, bf16[1440,2880]{1,0:T(8,128)(2,1)S(1)} %bitcast.22, bf16[1440,2880]{1,0:T(8,128)(2,1)S(1)} %bitcast.25, bf16[1440,2880]{1,0:T(8,128)(2,1)} %bitcast.28), custom_call_target="tpu_custom_call" | custom-call | flops 26542080000 | bytes 40000000 | tf_op jit(solution)/shard_map/pallas_call | solution.py:210
  140.5 53.7 %all_to_all.11 = bf16[128,57,2,128]{3,2,1,0:T(2,128)(2,1)S(1)} all-to-all(bf16[128,57,2,128]{3,2,1,0:T(2,128)(2,1)S(1)} %bitcast.16), channel_id=1, replica_groups=mesh['node'=16,'local'=8] {'node','local'}, dimensions={0} | all-to-all | bytes 7471104 | tf_op jit(solution)/shard_map/all_to_all | solution.py:288
  194.3 0.0 copy-done
  194.3 0.0 copy-done.1
  194.3 2.9 %shard_map.88 = (bf16[2880,128]{1,0:T(8,128)(2,1)}, f32[4,128]{1,0:T(4,128)}) custom-call(s32[4,128]{1,0:T(4,128)S(1)} %bitcast.18, f32[4,128]{1,0:T(4,128)S(1)} %bitcast.19, bf16[14592,128]{1,0:T(8,128)(2,1)S(1)} %bitcast.15), custom_call_target="tpu_custom_call" | custom-call | tf_op jit(solution)/shard_map/pallas_call | solution.py:272
  (2 shorter events, 0.0 us)
Async XLA Ops:
  0.6 105.1 %slice-start = ((s8[8478720]{0:T(1024)(128)(4,1)}), s8[4194304]{0:T(1024)(128)(4,1)S(1)}, s32[]{:S(2)}) async-start(s8[8478720]{0:T(1024)(128)(4,1)} %bitcast.20), calls=%async_computation.2 | async-start | bytes 8388608
  0.6 105.1 %slice-start.1 = ((s8[8478720]{0:T(1024)(128)(4,1)}), s8[4194304]{0:T(1024)(128)(4,1)S(1)}, s32[]{:S(2)}) async-start(s8[8478720]{0:T(1024)(128)(4,1)} %bitcast.20), calls=%async_computation.3 | async-start | bytes 8388608
  0.7 105.1 %slice-start.3 = ((s8[8478720]{0:T(1024)(128)(4,1)}), s8[4194304]{0:T(1024)(128)(4,1)S(1)}, s32[]{:S(2)}) async-start(s8[8478720]{0:T(1024)(128)(4,1)} %bitcast.23), calls=%async_computation.5 | async-start | bytes 8388608
  0.7 105.1 %slice-start.4 = ((s8[8478720]{0:T(1024)(128)(4,1)}), s8[4194304]{0:T(1024)(128)(4,1)S(1)}, s32[]{:S(2)}) async-start(s8[8478720]{0:T(1024)(128)(4,1)} %bitcast.23), calls=%async_computation.6 | async-start | bytes 8388608
  4.9 100.9 %slice-start.2 = ((s8[8478720]{0:T(1024)(128)(4,1)}), s8[90112]{0:T(1024)(128)(4,1)S(1)}, s32[]{:S(2)}) async-start(s8[8478720]{0:T(1024)(128)(4,1)} %bitcast.20), calls=%async_computation.4 | async-start | bytes 180224
  4.9 100.9 %slice-start.5 = ((s8[8478720]{0:T(1024)(128)(4,1)}), s8[90112]{0:T(1024)(128)(4,1)S(1)}, s32[]{:S(2)}) async-start(s8[8478720]{0:T(1024)(128)(4,1)} %bitcast.23), calls=%async_computation.7 | async-start | bytes 180224
  105.8 88.4 %copy-start = (s32[128,4]{0,1:T(4,128)S(1)}, s32[128,4]{0,1:T(4,128)}, u32[]{:S(2)}) copy-start(s32[128,4]{0,1:T(4,128)} %param.9) | copy-start | bytes 6148
  105.8 88.4 %copy-start.1 = (f32[128,4]{0,1:T(4,128)S(1)}, f32[128,4]{0,1:T(4,128)}, u32[]{:S(2)}) copy-start(f32[128,4]{0,1:T(4,128)} %param.10) | copy-start | bytes 6148

commit v5 on v4

--- a/solution.py
+++ b/solution.py
@@ -120,15 +120,19 @@
 
 def expert_kernel(
     tiles, pitch_in, pitch_out, in_ref, gate_ref, up_ref, down_hbm, out_ref,
-    rows_ref, pre_ref, upg_ref, down_ref, stage_ref, sem,
+    rows_ref, pre_ref, upg_ref, down_ref, stage_ref, sems,
 ):
     peers, rows_in, _ = in_ref.shape
     rows_out = out_ref.shape[0] // peers
     hidden, features = gate_ref.shape
     wide = SLOTS * peers
     chunks = [(lo, min(lo + 512, hidden)) for lo in range(0, hidden, 512)]
-    arrival = pltpu.make_async_copy(down_hbm, down_ref, sem)
-    arrival.start()
+    arrivals = [
+        pltpu.make_async_copy(down_hbm.at[pl.ds(lo, hi - lo)], down_ref.at[pl.ds(lo, hi - lo)], sems.at[c])
+        for c, (lo, hi) in enumerate(chunks)
+    ]
+    for arrival in arrivals:
+        arrival.start()
     whole = features // LANES
     first_row = [0, (SLOTS * tiles) // 16 * 16]
 
@@ -158,7 +162,7 @@
         if c == 0:
             for g in range(peers // GROUP):
                 unpack(1, g)
-            arrival.wait()
+        arrivals[c].wait()
         hidden_grad = lax.dot_general(
             rows_ref[1, :, :features], down_ref[lo:hi, :], NT, preferred_element_type=F32
         )
@@ -218,7 +222,7 @@
             pltpu.VMEM((wide, hidden), BF),
             pltpu.VMEM((hidden, features), BF),
             pltpu.VMEM((LANES * (rows_out + 7), LANES), F32),
-            pltpu.SemaphoreType.DMA,
+            pltpu.SemaphoreType.DMA((-(-hidden // 512),)),
         ],
         compiler_params=pltpu.CompilerParams(vmem_limit_bytes=EXPERT_LIMIT),
         cost_estimate=pl.CostEstimate(flops=flops, bytes_accessed=40_000_000, transcendentals=0),

time: 197 us -> 197 us (level)
  no operation moved by 1% of the time
where the time goes in v5:
time: 197 us
  blocking collectives  155 us (79%)
  Pallas kernels  41.3 us (21%)
    all_to_all x2, blocking collectives, exchange(): lax.all_to_all(messages, ('node', 'local'), split_axis=0, concat_axis=0,...  155 us
    pallas_call x1, Pallas kernels, expert(): pl.pallas_call(functools.partial(expert_kernel, tiles, pitch_in, pitch_ou...  34.2 us
    pallas_call x1, Pallas kernels, dispatch(): pl.pallas_call(functools.partial(dispatch_kernel, tiles, pitch), in_specs...  4.21 us

profile of v5, /device:TPU:1, one launch (start us, length us, event | category | flops | bytes accessed | tf_op | source)
XLA Modules:
  0.0 196.7 jit_solution(16398980761990773485)
XLA Ops:
  0.6 0.0 slice-start
  0.6 0.0 slice-start.1
  0.7 0.0 slice-start.3
  0.7 0.0 slice-start.4
  0.7 4.2 %shard_map.86 = bf16[128,232,128]{2,1,0:T(8,128)(2,1)S(1)} custom-call(s32[4,128]{1,0:T(4,128)} %bitcast.17, bf16[2880,128]{1,0:T(8,128)(2,1)} %bitcast.26, bf16[2880,128]{1,0:T(8,128)(2,1)} %bitcast.27), custom_call_target="tpu_custom_call" | custom-call | tf_op jit(solution)/shard_map/pallas_call | solution.py:105
  4.9 0.0 slice-start.2
  4.9 0.0 slice-start.5
  4.9 100.8 %all_to_all.10.in_ref = bf16[128,232,128]{2,1,0:T(8,128)(2,1)S(1)} all-to-all(bf16[128,232,128]{2,1,0:T(8,128)(2,1)S(1)} %shard_map.86), channel_id=1, replica_groups=mesh['node'=16,'local'=8] {'node','local'}, dimensions={0} | all-to-all | bytes 15204352 | tf_op jit(solution)/shard_map/all_to_all | solution.py:292
  105.8 0.0 slice-done
  105.8 0.0 slice-done.1
  105.8 0.0 slice-done.3
  105.8 0.0 slice-done.4
  105.8 0.0 slice-done.2
  105.8 0.0 slice-done.5
  105.8 0.0 copy-start
  105.8 0.0 copy-start.1
  105.9 34.2 %shard_map.87 = bf16[14592,128]{1,0:T(8,128)(2,1)S(1)} custom-call(bf16[128,232,128]{2,1,0:T(8,128)(2,1)S(1)} %all_to_all.10.in_ref, bf16[1440,2880]{1,0:T(8,128)(2,1)S(1)} %bitcast.22, bf16[1440,2880]{1,0:T(8,128)(2,1)S(1)} %bitcast.25, bf16[1440,2880]{1,0:T(8,128)(2,1)} %bitcast.28), custom_call_target="tpu_custom_call" | custom-call | flops 26542080000 | bytes 40000000 | tf_op jit(solution)/shard_map/pallas_call | solution.py:214
  140.1 53.7 %all_to_all.11 = bf16[128,57,2,128]{3,2,1,0:T(2,128)(2,1)S(1)} all-to-all(bf16[128,57,2,128]{3,2,1,0:T(2,128)(2,1)S(1)} %bitcast.16), channel_id=1, replica_groups=mesh['node'=16,'local'=8] {'node','local'}, dimensions={0} | all-to-all | bytes 7471104 | tf_op jit(solution)/shard_map/all_to_all | solution.py:292
  193.8 0.0 copy-done
  193.8 0.0 copy-done.1
  193.8 2.9 %shard_map.88 = (bf16[2880,128]{1,0:T(8,128)(2,1)}, f32[4,128]{1,0:T(4,128)}) custom-call(s32[4,128]{1,0:T(4,128)S(1)} %bitcast.18, f32[4,128]{1,0:T(4,128)S(1)} %bitcast.19, bf16[14592,128]{1,0:T(8,128)(2,1)S(1)} %bitcast.15), custom_call_target="tpu_custom_call" | custom-call | tf_op jit(solution)/shard_map/pallas_call | solution.py:276
  (2 shorter events, 0.0 us)
Async XLA Ops:
  0.6 105.1 %slice-start = ((s8[8478720]{0:T(1024)(128)(4,1)}), s8[4194304]{0:T(1024)(128)(4,1)S(1)}, s32[]{:S(2)}) async-start(s8[8478720]{0:T(1024)(128)(4,1)} %bitcast.20), calls=%async_computation.2 | async-start | bytes 8388608
  0.6 105.1 %slice-start.1 = ((s8[8478720]{0:T(1024)(128)(4,1)}), s8[4194304]{0:T(1024)(128)(4,1)S(1)}, s32[]{:S(2)}) async-start(s8[8478720]{0:T(1024)(128)(4,1)} %bitcast.20), calls=%async_computation.3 | async-start | bytes 8388608
  0.7 105.1 %slice-start.3 = ((s8[8478720]{0:T(1024)(128)(4,1)}), s8[4194304]{0:T(1024)(128)(4,1)S(1)}, s32[]{:S(2)}) async-start(s8[8478720]{0:T(1024)(128)(4,1)} %bitcast.23), calls=%async_computation.5 | async-start | bytes 8388608
  0.7 105.1 %slice-start.4 = ((s8[8478720]{0:T(1024)(128)(4,1)}), s8[4194304]{0:T(1024)(128)(4,1)S(1)}, s32[]{:S(2)}) async-start(s8[8478720]{0:T(1024)(128)(4,1)} %bitcast.23), calls=%async_computation.6 | async-start | bytes 8388608
  4.9 100.9 %slice-start.2 = ((s8[8478720]{0:T(1024)(128)(4,1)}), s8[90112]{0:T(1024)(128)(4,1)S(1)}, s32[]{:S(2)}) async-start(s8[8478720]{0:T(1024)(128)(4,1)} %bitcast.20), calls=%async_computation.4 | async-start | bytes 180224
  4.9 100.9 %slice-start.5 = ((s8[8478720]{0:T(1024)(128)(4,1)}), s8[90112]{0:T(1024)(128)(4,1)S(1)}, s32[]{:S(2)}) async-start(s8[8478720]{0:T(1024)(128)(4,1)} %bitcast.23), calls=%async_computation.7 | async-start | bytes 180224
  105.8 88.0 %copy-start = (s32[128,4]{0,1:T(4,128)S(1)}, s32[128,4]{0,1:T(4,128)}, u32[]{:S(2)}) copy-start(s32[128,4]{0,1:T(4,128)} %param.9) | copy-start | bytes 6148
  105.8 88.0 %copy-start.1 = (f32[128,4]{0,1:T(4,128)S(1)}, f32[128,4]{0,1:T(4,128)}, u32[]{:S(2)}) copy-start(f32[128,4]{0,1:T(4,128)} %param.10) | copy-start | bytes 6148
